TPU v7x, 128 devices: a whole 4x4x4 slice. The times are simulated.
128 devices in a mesh: atm: 8 (over y, core), ocn: 16 (over z, x).
Axes of the slice: x: 4, y: 4, z: 4, core: 2. Of those that a mesh axis runs over, the one named last changes fastest.
Arguments:
- atm_state: float32 [2, 72, 256, 2048], P(None, None, 'atm', 'ocn'), may hold values from -6 to 6
- ocn_state: float32 [4, 4, 512, 2048], P(None, None, 'atm', 'ocn'), may hold values from -6 to 6
- land: int32 [512, 2048], P('atm', 'ocn'), may hold values 0 or 1
- ocn_kappa: float32 [512, 2048], P('atm', 'ocn'), may hold values from 0.05 to 0.24
- partner: int32 [16, 512, 1], P('ocn', 'atm'), may hold values from 0 to 15; in each aligned block of 64 rows (0 to 63, 64 to 127, ..., all dimensions but the last counted through in order) at most 8 rows name the same one
- partner_row: int32 [16, 512, 1], P('ocn', 'atm'), may hold values from 0 to 31
- remap_up: float32 [512, 2048, 128], P('atm', 'ocn'), may hold values from -0.375 to 0.375
- remap_down: float32 [512, 2048, 128], P('atm', 'ocn'), may hold values from -0.5 to 0.5
- surface_mix: float32 [4, 16], replicated, may hold values from -1.5 to 1.5
- drag: float32 [256, 2048], P('atm', 'ocn'), may hold values from 0.1 to 1
- level_kappa: float32 [72], replicated, may hold values from 0.05 to 0.2
- vertical_mix: float32 [72, 72], replicated, may hold values from -0.2 to 0.8
- depth_gain: float32 [4], replicated, may hold values from 0.5 to 2
Outputs:
- atm_out: float32 [2, 72, 256, 2048], P(None, None, 'atm', 'ocn')
- ocn_out: float32 [4, 4, 512, 2048], P(None, None, 'atm', 'ocn')
Inputs may be any that keep to these rules, and one draw needn't show every extreme that they name: `partner`: of the 64 ocean blocks of one device at most 8 have partners on one atmosphere tile, and some device has exactly 8 on one tile.
All inputs are finite; a program needn't handle non-finite values. No bound on the sum of `land` on one device may be relied on, other than what follows from the above.
Results may differ from a plain program's by a relative error of at most 0.00012.
Values sent between devices are 32-bit elements; how exact they have to be, the bound alone decides.
A program may use at most 128 MiB of HBM per device.

v0:
```python
import functools

import jax
import jax.numpy as jnp
from jax import lax
from jax.experimental import pallas as pl
from jax.experimental.pallas import tpu as pltpu
from jax.sharding import PartitionSpec as P

f32 = jnp.float32
bf16 = jnp.bfloat16
LEV = 72
ASTEPS = 6
OSTEPS = 4
ROWS = 32
BLK = 64
W = 128
EXT = ROWS + 2 * ASTEPS
PAIRS = EXT // 2


def mm(a, b, dims=((1,), (0,)), precision=None):
    return lax.dot_general(a, b, (dims, ((), ())), precision=precision, preferred_element_type=f32)


def high(x):
    return x.astype(bf16).astype(f32)


def pick(onehot, x):
    left = onehot.astype(bf16)
    hi = high(x)
    rest = x - hi
    mid = high(rest)
    low = rest - mid
    return mm(left, hi.astype(bf16)) + mm(left, mid.astype(bf16)) + mm(left, low.astype(bf16))


def lanes(shape):
    return lax.broadcasted_iota(jnp.int32, shape, len(shape) - 1)


def rows_of(shape):
    return lax.broadcasted_iota(jnp.int32, shape, len(shape) - 2)


def rolled(x, shift, axis=1):
    if isinstance(shift, int):
        shift = shift % x.shape[axis]
        if shift == 0:
            return x
    return pltpu.roll(x, shift, axis)


def kernel(
    na, no, cap,
    atm, atm_flat, ocn, land, kappa, partner, prow, up, down, smix, drag, lk, vm, gain,
    atm_out, ocn_out,
    a_flat, a_top, a_bot, top_flat, bot_flat, u_own, up_v, down_v,
    r_out, l_out, d_out, l_in, r_in, d_in,
    ob, oe, ob_top, ob_bot, oe_l, oe_r, oe_c,
    rid_out, rid_in, c_out, c_in, p_out, p_in,
    fx, fx_l, fx_r, fx_t, fx_b, fx_c,
    mx, cb, w_s, wf_s, gs, out_a, out_o, us, st,
    p0, p1, p2, p3, p4, p5, p6,
    s0, s1, s2, s3, s4, s5, s6,
    loc, hs, hr, ps, pr,
):
    me_a = lax.axis_index("atm")
    me_o = lax.axis_index("ocn")
    above, below = lax.rem(me_a + na - 1, na), lax.rem(me_a + 1, na)
    left, right = lax.rem(me_o + no - 1, no), lax.rem(me_o + 1, no)
    slots = no * cap
    pm = (p0, p1, p2, p3, p4, p5, p6)
    sm = (s0, s1, s2, s3, s4, s5, s6)

    def local(src, dst, i):
        c = pltpu.make_async_copy(src, dst, loc.at[i])
        c.start()
        return c

    g_ocn = local(ocn, u_own, 0)
    chunks = 4
    part = BLK // chunks
    g_up = [local(up.at[pl.ds(i * part, part)], up_v.at[pl.ds(i * part, part)], 1 + i) for i in range(chunks)]
    g_atm = local(atm_flat, a_flat, 5)
    g_down = local(down, down_v, 6)

    barrier = pltpu.get_barrier_semaphore()
    greeted = [(me_a, lax.rem(me_o + d, no)) for d in range(1, no)]
    greeted += [(r, c) for r in (above, below) for c in (me_o, left, right)]
    for r, c in greeted:
        pl.semaphore_signal(barrier, inc=1, device_id={"atm": r, "ocn": c}, device_id_type=pl.DeviceIdType.MESH)
    pl.semaphore_wait(barrier, len(greeted))

    sent = []

    def send(src, dst, i, r, c):
        d = pltpu.make_async_remote_copy(
            src_ref=src, dst_ref=dst, send_sem=hs.at[i], recv_sem=hr.at[i],
            device_id={"atm": r, "ocn": c}, device_id_type=pl.DeviceIdType.MESH,
        )
        d.start()
        sent.append(d)
        return d

    def spread(src, dst, group):
        made = []
        for d in range(1, no):
            peer = lax.rem(me_o + d, no)
            c = pltpu.make_async_remote_copy(
                src_ref=src.at[pl.ds(pl.multiple_of(peer * cap, 8), cap)],
                dst_ref=dst.at[pl.ds(pl.multiple_of(me_o * cap, 8), cap)],
                send_sem=ps.at[group, d], recv_sem=pr.at[group, d],
                device_id={"atm": me_a, "ocn": peer}, device_id_type=pl.DeviceIdType.MESH,
            )
            c.start()
            sent.append(c)
            made.append(c)
        return made

    def arrive(made):
        for c in made:
            c.wait_recv()

    mine_rows = pl.ds(pl.multiple_of(me_o * cap, 8), cap)

    h_bot = send(atm.at[:, pl.ds(0, 8)], a_bot, 0, above, me_o)
    h_top = send(atm.at[:, pl.ds(ROWS - 8, 8)], a_top, 1, below, me_o)

    t_row = partner[...].astype(f32)
    r_row = prow[...].astype(f32)
    ii, jj = rows_of((BLK, BLK)), lanes((BLK, BLK))
    t_all = jnp.broadcast_to(t_row, (BLK, BLK))
    t_col = jnp.sum(jnp.where(ii == jj, t_all, 0.0), axis=1, keepdims=True)
    same = t_col == t_all
    pos_row = jnp.sum(jnp.where(same & (ii < jj), 1.0, 0.0), axis=0, keepdims=True)
    pos_col = jnp.sum(jnp.where(same & (jj < ii), 1.0, 0.0), axis=1, keepdims=True)
    slot_row = t_row * cap + pos_row
    slot_col = t_col * cap + pos_col
    chosen = jnp.where(rows_of((slots, BLK)).astype(f32) == slot_row, 1.0, 0.0)
    chosen_t = jnp.where(lanes((BLK, slots)).astype(f32) == slot_col, 1.0, 0.0)
    rid = jnp.sum(chosen * (r_row + 1.0), axis=1, keepdims=True) - 1.0
    rid_out[...] = jnp.broadcast_to(rid, (slots, W))
    g_rid = spread(rid_out, rid_in, 0)

    lf = land[...].astype(f32)
    g_ocn.wait()
    for k in range(4):
        total = smix[k, 0] * u_own[0]
        for c in range(1, 16):
            total = total + smix[k, c] * u_own[c]
        total = total * lf
        hi = high(total)
        mx[pl.ds(k, BLK, stride=8), :] = hi
        mx[pl.ds(4 + k, BLK, stride=8), :] = total - hi

    def remap(b, weights, transposed):
        block = weights[b]
        hi = high(block)
        parts = (hi.astype(bf16), (block - hi).astype(bf16))
        vec = mx[pl.ds(pl.multiple_of(b * 8, 8), 8), :].astype(bf16)
        if transposed:
            res = mm(vec, jnp.concatenate(parts, 0), ((1,), (1,)))
        else:
            res = mm(vec, jnp.concatenate(parts, 1))
        first = res[:, :W]
        cb[pl.ds(pl.multiple_of(b * 8, 8), 8), :] = first + rolled(first, 4, 0) + res[:, W:]

    for i in range(chunks):
        g_up[i].wait()
        lax.fori_loop(i * part, (i + 1) * part, lambda b, _: (remap(b, up_v, False), 0)[1], 0, unroll=4)
    fields = jnp.concatenate([cb[pl.ds(k, BLK, stride=8), :] for k in range(4)], 1)
    c_out[...] = pick(chosen, fields)
    g_c = spread(c_out, c_in, 1)

    for c in range(16):
        ob[c] = u_own[c]
    ob[16] = lf
    ob[17] = kappa[...]
    lane64 = lanes((BLK, W))
    edge = jnp.zeros((BLK, W), f32)
    for c in range(16):
        edge = jnp.where(lane64 // 8 == c, rolled(u_own[c], 8 * c + 4), edge)
    oe[0] = edge
    oe[1] = jnp.where(lane64 // 8 == 0, rolled(lf, 4), rolled(kappa[...], 12))
    h_ob = [
        send(ob.at[:, pl.ds(0, 8)], ob_bot, 2, above, me_o),
        send(ob.at[:, pl.ds(BLK - 8, 8)], ob_top, 3, below, me_o),
        send(oe, oe_r, 4, me_a, left),
        send(oe, oe_l, 5, me_a, right),
        send(oe.at[:, pl.ds(BLK - 8, 8)], oe_c.at[0], 6, below, right),
        send(oe.at[:, pl.ds(BLK - 8, 8)], oe_c.at[1], 7, below, left),
        send(oe.at[:, pl.ds(0, 8)], oe_c.at[2], 8, above, right),
        send(oe.at[:, pl.ds(0, 8)], oe_c.at[3], 9, above, left),
    ]

    g_atm.wait()
    lane = lanes((LEV, W))

    def own_row(v, x):
        return a_flat[pl.ds(v * LEV * ROWS + x, LEV, stride=ROWS), :]

    for half in range(2):
        for v in range(2):
            def gather(i, carry):
                to_r, to_l = carry
                row = own_row(v, half * 16 + i)
                here = lane // 8 == i
                return (
                    jnp.where(here, rolled(row, lax.rem(8 * i + 6, W)), to_r),
                    jnp.where(here, rolled(row, 8 * i), to_l),
                )
            to_r, to_l = lax.fori_loop(0, 16, gather, (jnp.zeros((LEV, W), f32), jnp.zeros((LEV, W), f32)))
            r_out[half, v] = to_r
            l_out[half, v] = to_l
    for n, buf in ((0, r_out), (2, l_out)):
        d_out[n] = jnp.where(lane < 64, buf[0, 0], rolled(buf[0, 1], 64))
        d_out[n + 1] = jnp.where(lane < 64, rolled(buf[1, 0], 64), buf[1, 1])
    h_e = [
        send(r_out, l_in, 10, me_a, right),
        send(l_out, r_in, 11, me_a, left),
        send(d_out.at[1], d_in.at[0], 12, below, right),
        send(d_out.at[3], d_in.at[1], 13, below, left),
        send(d_out.at[0], d_in.at[2], 14, above, right),
        send(d_out.at[2], d_in.at[3], 15, above, left),
    ]

    exact = lax.Precision.HIGHEST
    rate = lk[...]
    zpad = jnp.zeros((LEV, W - LEV), f32)
    ca = jnp.concatenate([vm[...] * (1.0 - 4.0 * rate), zpad], 1)
    cc = jnp.concatenate([vm[...] * rate, zpad], 1)
    lhs = jnp.concatenate([ca, cc], 0)[:, :LEV]
    q = mm(lhs, jnp.concatenate([ca, cc], 1), precision=exact)
    q0, q1, q2 = q[:LEV, :W], q[:LEV, W:] + q[LEV:, :W], q[LEV:, W:]
    t = mm(lhs, jnp.concatenate([q0, q1, q2], 1), precision=exact)
    cubes = (
        t[:LEV, :W],
        t[:LEV, W:2 * W] + t[LEV:, :W],
        t[:LEV, 2 * W:] + t[LEV:, W:2 * W],
        t[LEV:, 2 * W:],
    )
    t = mm(jnp.concatenate(cubes, 0)[:, :LEV], jnp.concatenate(cubes, 1), precision=exact)
    wide = []
    column = jnp.zeros((LEV, W), f32)
    for k in range(7):
        m = None
        for i in range(max(0, k - 3), min(3, k) + 1):
            piece = t[LEV * i:LEV * (i + 1), W * (k - i):W * (k - i + 1)]
            m = piece if m is None else m + piece
        hi = high(m)
        z = jnp.zeros((LEV, W), f32)
        hi2 = jnp.concatenate([hi, z], 1)
        wide.append(hi2 + rolled(hi2, 80) + rolled(jnp.concatenate([m - hi, z], 1), 160))
        column = jnp.where(lane == k, rolled(m, k - (LEV - 1)), column)
    wide.append(jnp.zeros((8, 2 * W), f32))
    w_s[...] = jnp.concatenate(wide, 0)[:, :240].astype(bf16)
    chi = high(column)
    wf = chi + rolled(chi, 8) + rolled(column - chi, 16)
    wf_s[...] = jnp.concatenate([wf, jnp.zeros((8, W), f32)], 0)[:, :32].astype(bf16)

    def powers(x):
        hi = high(x)
        z = jnp.zeros((8, 2 * W), f32)
        h = jnp.concatenate([hi, z], 0).astype(bf16)
        m = jnp.concatenate([x - hi, z], 0).astype(bf16)
        return mm(w_s[...], jnp.concatenate([h, m, h], 0))

    def put_row(r, x):
        res = powers(x)
        for k in range(7):
            pm[k][r] = res[LEV * k:LEV * (k + 1)]

    def own_body(x, _):
        put_row(x + ASTEPS, jnp.concatenate([own_row(0, x), own_row(1, x)], 1))
        return 0

    lax.fori_loop(0, ROWS // 2, own_body, 0, unroll=2)

    rid_in[mine_rows] = rid_out[mine_rows]
    c_in[mine_rows] = c_out[mine_rows]
    arrive(g_rid)
    place_t = jnp.where(rid_in[...] == lanes((slots, W)).astype(f32), 1.0, 0.0)
    place = place_t.T[:ROWS]
    arrive(g_c)
    mixed = pick(place, c_in[...])
    flux = []
    for k in range(4):
        flux.append(drag[...] * (mixed[:, W * k:W * (k + 1)] - a_flat[pl.ds(((k % 2) * LEV + LEV - 1) * ROWS, ROWS), :]))
    p_out[...] = pick(place_t[:, :ROWS], jnp.concatenate(flux, 1))
    g_p = spread(p_out, p_in, 2)
    fx[0] = flux[0]
    fx[1] = flux[1]
    h_f = [
        send(fx, fx_r, 16, me_a, left),
        send(fx, fx_l, 17, me_a, right),
        send(fx.at[:, pl.ds(0, 8)], fx_b, 18, above, me_o),
        send(fx.at[:, pl.ds(ROWS - 8, 8)], fx_t, 19, below, me_o),
        send(fx.at[:, pl.ds(ROWS - 8, 8)], fx_c.at[0], 20, below, right),
        send(fx.at[:, pl.ds(ROWS - 8, 8)], fx_c.at[1], 21, below, left),
        send(fx.at[:, pl.ds(0, 8)], fx_c.at[2], 22, above, right),
        send(fx.at[:, pl.ds(0, 8)], fx_c.at[3], 23, above, left),
    ]

    lax.fori_loop(ROWS // 2, ROWS, own_body, 0, unroll=2)

    h_top.wait_recv()
    h_bot.wait_recv()

    top_flat[...] = jnp.where(me_a > 0, a_top[...], 0.0).reshape(2 * LEV * 8, W)
    bot_flat[...] = jnp.where(me_a < na - 1, a_bot[...], 0.0).reshape(2 * LEV * 8, W)

    def beside_row(flat, v, x):
        return flat[pl.ds(v * LEV * 8 + x, LEV, stride=8), :]

    def beside_body(x, _):
        put_row(x, jnp.concatenate([beside_row(top_flat, 0, x + 2), beside_row(top_flat, 1, x + 2)], 1))
        put_row(x + ROWS + ASTEPS, jnp.concatenate([beside_row(bot_flat, 0, x), beside_row(bot_flat, 1, x)], 1))
        return 0

    lax.fori_loop(0, ASTEPS, beside_body, 0)

    arrive(h_e)

    @pl.when(me_o == 0)
    def _():
        l_in[...] = jnp.zeros_like(l_in)
        d_in[0] = jnp.zeros((LEV, W), f32)
        d_in[2] = jnp.zeros((LEV, W), f32)

    @pl.when(me_o == no - 1)
    def _():
        r_in[...] = jnp.zeros_like(r_in)
        d_in[1] = jnp.zeros((LEV, W), f32)
        d_in[3] = jnp.zeros((LEV, W), f32)

    @pl.when(me_a == 0)
    def _():
        d_in[0] = jnp.zeros((LEV, W), f32)
        d_in[1] = jnp.zeros((LEV, W), f32)

    @pl.when(me_a == na - 1)
    def _():
        d_in[2] = jnp.zeros((LEV, W), f32)
        d_in[3] = jnp.zeros((LEV, W), f32)

    def strip(own0, own1, lefts, rights, place0, place1):
        out = jnp.where(lane < 12, own0, rolled(own0, 64))
        out = jnp.where(lane >= 122, rolled(lefts[0], lax.rem(122 + W - place0, W)), out)
        out = jnp.where((lane >= 64) & (lane < 70), rolled(rights[0], lax.rem(64 + W - place0, W)), out)
        out = jnp.where((lane >= 32) & (lane < 44), rolled(own1, 32), out)
        out = jnp.where((lane >= 84) & (lane < 96), rolled(own1, 96), out)
        out = jnp.where((lane >= 26) & (lane < 32), rolled(lefts[1], lax.rem(26 + W - place1, W)), out)
        return jnp.where((lane >= 96) & (lane < 102), rolled(rights[1], lax.rem(96 + W - place1, W)), out)

    def put_pair(pair, x):
        res = powers(x)
        for k in range(7):
            sm[k][pair + 1] = res[LEV * k:LEV * (k + 1)]

    for half in range(2):
        def strip_body(i, _):
            made = []
            for h in range(2):
                n = 2 * i + h
                x = half * 16 + n
                made.append(strip(
                    own_row(0, x), own_row(1, x),
                    (l_in[half, 0], l_in[half, 1]), (r_in[half, 0], r_in[half, 1]), 8 * n, 8 * n,
                ))
            put_pair(half * 8 + i + ASTEPS // 2, jnp.concatenate(made, 1))
            return 0
        lax.fori_loop(0, 8, strip_body, 0)
    for flat, first, base, corner in ((top_flat, 2, 0, 0), (bot_flat, 0, (ROWS + ASTEPS) // 2, 2)):
        def corner_body(i, _):
            made = []
            for h in range(2):
                x = 2 * i + h + first
                made.append(strip(
                    beside_row(flat, 0, x), beside_row(flat, 1, x),
                    (d_in[corner], d_in[corner]), (d_in[corner + 1], d_in[corner + 1]), 8 * x, 8 * x + 64,
                ))
            put_pair(base + i, jnp.concatenate(made, 1))
            return 0
        lax.fori_loop(0, ASTEPS // 2, corner_body, 0)
    for k in range(7):
        sm[k][0] = jnp.zeros((LEV, 2 * W), f32)
        sm[k][PAIRS + 1] = jnp.zeros((LEV, 2 * W), f32)

    lane1 = lanes((1, W))
    outside_l = ((lane1 >= 122) | ((lane1 >= 26) & (lane1 < 32))) & (me_o == 0)
    outside_r = (((lane1 >= 64) & (lane1 < 70)) | ((lane1 >= 96) & (lane1 < 102))) & (me_o == no - 1)
    inside = jnp.where(outside_l | outside_r, 0.0, 1.0)

    for k in range(ASTEPS - 1, -1, -1):
        src, dst = pm[k + 1], pm[k]
        first = ASTEPS - k
        count = EXT - 2 * first
        group = 4 if count % 4 == 0 else 2

        def main_body(i, _):
            r = first + i * group
            for h in range(2):
                sl = slice(W * h, W * (h + 1))
                near = [src[r - 1 + n, :, sl] for n in range(group + 2)]
                made = []
                for n in range(group):
                    c = near[n + 1]
                    made.append(dst[r + n, :, sl] + ((near[n] + near[n + 2]) + (rolled(c, 1) + rolled(c, W - 1))))
                for n in range(group):
                    dst[r + n, :, sl] = made[n]
            return 0
        lax.fori_loop(0, count // group, main_body, 0)

        ssrc, sdst = sm[k + 1], sm[k]

        def strip_step(i, _):
            q = i + first // 2
            a0, a1 = ssrc[q + 1, :, :W], ssrc[q + 1, :, W:]
            made0 = (ssrc[q, :, W:] + a1) + (rolled(a0, 1) + rolled(a0, W - 1))
            made1 = (ssrc[q + 2, :, :W] + a0) + (rolled(a1, 1) + rolled(a1, W - 1))
            sdst[q + 1, :, :W] = sdst[q + 1, :, :W] + made0 * inside
            sdst[q + 1, :, W:] = sdst[q + 1, :, W:] + made1 * inside
            return 0
        lax.fori_loop(0, PAIRS - 2 * (first // 2), strip_step, 0)

        if k:
            @pl.when(me_a == 0)
            def _():
                for r in range(ASTEPS):
                    dst[r] = jnp.zeros((LEV, 2 * W), f32)
                for r in range(ASTEPS // 2):
                    sdst[r + 1] = jnp.zeros((LEV, 2 * W), f32)

            @pl.when(me_a == na - 1)
            def _():
                for r in range(ASTEPS):
                    dst[ROWS + ASTEPS + r] = jnp.zeros((LEV, 2 * W), f32)
                for r in range(ASTEPS // 2):
                    sdst[(ROWS + ASTEPS) // 2 + r + 1] = jnp.zeros((LEV, 2 * W), f32)

    arrive(h_ob)
    tall = BLK + 16
    rr = rows_of((tall, W))
    row_in = ((rr >= 8) | (me_a > 0)) & ((rr < BLK + 8) | (me_a < na - 1))
    lane_t = lanes((tall, W))

    def tall_of(c):
        return jnp.concatenate([ob_top[c], ob[c], ob_bot[c]], 0)

    def tall_edge(n, side):
        body = oe_l[n] if side == 0 else oe_r[n]
        return jnp.concatenate([oe_c[side, n], body, oe_c[2 + side, n]], 0)

    def neighbours(x):
        return (rolled(x, 1, 0) + rolled(x, tall - 1, 0)) + (rolled(x, 1) + rolled(x, W - 1))

    def stepped(x, c0, c1):
        for _ in range(OSTEPS):
            x = c0 * x + c1 * neighbours(x)
        return x

    sea = jnp.where(row_in, tall_of(16), 0.0)
    kap = tall_of(17)
    c1 = kap * sea
    c0 = sea - c1 * neighbours(sea)

    def edges(own, l_edge, r_edge, at, slot):
        out = jnp.where(lane_t < 32 * slot + 4, rolled(l_edge, 32 * slot - at), rolled(own, 32 * slot + 4))
        out = jnp.where(lane_t >= 32 * slot + 16, rolled(own, 32 * slot + 24), out)
        return jnp.where(lane_t >= 32 * slot + 24, rolled(r_edge, 32 * slot + 20 - at), out)

    in_l = (lane_t >= 4) | (me_o > 0)
    in_r = (lane_t < 24) | (me_o < no - 1)
    used = ((lane_t < 12) | ((lane_t >= 16) & (lane_t < 28))) & in_l & in_r & row_in
    tl, tr = tall_edge(1, 0), tall_edge(1, 1)
    e_sea = jnp.where(used, edges(tall_of(16), tl, tr, 0, 0), 0.0)
    e_kap = jnp.where(used, edges(kap, tl, tr, 8, 0), 0.0)

    def four(x):
        return (x + rolled(x, 32)) + (rolled(x, 64) + rolled(x, 96))

    e_sea, e_kap = four(e_sea), four(e_kap)
    e1 = e_kap * e_sea
    e0 = e_sea - e1 * neighbours(e_sea)
    ul, ur = tall_edge(0, 0), tall_edge(0, 1)
    for g in range(4):
        total = edges(tall_of(4 * g), ul, ur, 32 * g, 0)
        for s in range(1, 4):
            c = 4 * g + s
            total = jnp.where(lane_t >= 32 * s, edges(tall_of(c), ul, ur, 8 * c, s), total)
        st[g] = stepped(e_sea * total, e0, e1)[8:8 + BLK]
    for c in range(16):
        mid = stepped(sea * tall_of(c), c0, c1)[8:8 + BLK]
        e = st[c // 4]
        base = 32 * (c % 4)
        mid = jnp.where(lane64 < 4, rolled(e, -base - 4), mid)
        mid = jnp.where(lane64 >= W - 4, rolled(e, 104 - base), mid)
        us[c] = mid + (1.0 - lf) * u_own[c]

    p_in[mine_rows] = p_out[mine_rows]
    arrive(g_p)
    mine = pick(chosen_t, p_in[...])
    for k in range(4):
        x = mine[:, W * k:W * (k + 1)]
        hi = high(x)
        mx[pl.ds(k, BLK, stride=8), :] = hi
        mx[pl.ds(4 + k, BLK, stride=8), :] = x - hi
    g_down.wait()
    lax.fori_loop(0, BLK, lambda b, _: (remap(b, down_v, True), 0)[1], 0, unroll=4)
    for v in range(4):
        term = cb[pl.ds(v, BLK, stride=8), :] * lf
        for n in range(4):
            out_o[4 * v + n] = us[4 * v + n] + gain[0, n] * term
    g_oo = local(out_o, ocn_out, 0)

    arrive(h_f)
    rows48, lanes384 = rows_of((ROWS + 16, 3 * W)), lanes((ROWS + 16, 3 * W))
    grid_in = ((rows48 >= 8) | (me_a > 0)) & ((rows48 < ROWS + 8) | (me_a < na - 1))
    grid_in = grid_in & ((lanes384 >= W) | (me_o > 0)) & ((lanes384 < 2 * W) | (me_o < no - 1))
    grid_in = jnp.where(grid_in, 1.0, 0.0)
    for v in range(2):
        cur = jnp.concatenate([
            jnp.concatenate([fx_c[0, v], fx_t[v], fx_c[1, v]], 1),
            jnp.concatenate([fx_l[v], fx[v], fx_r[v]], 1),
            jnp.concatenate([fx_c[2, v], fx_b[v], fx_c[3, v]], 1),
        ], 0) * grid_in
        for j in range(8):
            if j == 7:
                gs[v, pl.ds(j, ROWS, stride=8), :] = jnp.zeros((ROWS, W), f32)
                break
            gs[v, pl.ds(j, ROWS, stride=8), :] = cur[8:8 + ROWS, W:2 * W]
            if j < 6:
                cur = grid_in * (
                    (rolled(cur, 1, 0) + rolled(cur, ROWS + 15, 0)) + (rolled(cur, 1) + rolled(cur, 3 * W - 1))
                )

    def final_body(i, _):
        for h in range(2):
            x = 2 * i + h
            at = pl.ds(pl.multiple_of(8 * x, 8), 8)
            g = jnp.concatenate([gs[0, at, :], gs[1, at, :]], 1)
            hi = high(g)
            rhs = jnp.concatenate([hi, g - hi, hi, jnp.zeros((8, 2 * W), f32)], 0).astype(bf16)
            extra = mm(wf_s[...], rhs)[:LEV]
            e = s0[i + ASTEPS // 2 + 1, :, W * h:W * (h + 1)]
            for v in range(2):
                res = p0[x + ASTEPS, :, W * v:W * (v + 1)]
                res = jnp.where(lane < 6, rolled(e, -32 * v), res)
                res = jnp.where(lane >= 122, rolled(e, 64 - 32 * v), res)
                out_a[pl.ds(v * LEV * ROWS + x, LEV, stride=ROWS), :] = res + extra[:, W * v:W * (v + 1)]
        return 0

    lax.fori_loop(0, ROWS // 2, final_body, 0)
    g_ao = local(out_a, atm_out, 5)
    for c in sent:
        c.wait_send()
    g_oo.wait()
    g_ao.wait()


def shards(
    na, no,
    atm_state, ocn_state, land, ocn_kappa, partner, partner_row, remap_up, remap_down,
    surface_mix, drag, level_kappa, vertical_mix, depth_gain,
):
    cap = max(2, 2 * BLK // no)
    slots = no * cap
    vmem = pl.BlockSpec(memory_space=pltpu.VMEM)
    smem = pl.BlockSpec(memory_space=pltpu.SMEM)
    hbm = pl.BlockSpec(memory_space=pl.ANY)

    def v(*shape, dtype=f32):
        return pltpu.VMEM(shape, dtype)

    scratch = [
        v(2 * LEV * ROWS, W), v(2 * LEV, 8, W), v(2 * LEV, 8, W), v(2 * LEV * 8, W), v(2 * LEV * 8, W), v(16, BLK, W), v(BLK, W, W), v(BLK, W, W),
        v(2, 2, LEV, W), v(2, 2, LEV, W), v(4, LEV, W), v(2, 2, LEV, W), v(2, 2, LEV, W), v(4, LEV, W),
        v(18, BLK, W), v(2, BLK, W), v(18, 8, W), v(18, 8, W), v(2, BLK, W), v(2, BLK, W), v(4, 2, 8, W),
        v(slots, W), v(slots, W), v(slots, 4 * W), v(slots, 4 * W), v(slots, 4 * W), v(slots, 4 * W),
        v(2, ROWS, W), v(2, ROWS, W), v(2, ROWS, W), v(2, 8, W), v(2, 8, W), v(4, 2, 8, W),
        v(BLK * 8, W), v(BLK * 8, W), v(512, 240, dtype=bf16), v(80, 32, dtype=bf16), v(2, ROWS * 8, W),
        v(2 * LEV * ROWS, W), v(16, BLK, W), v(16, BLK, W), v(4, BLK, W),
    ]
    scratch += [v(EXT, LEV, 2 * W) for _ in range(7)]
    scratch += [v(PAIRS + 2, LEV, 2 * W) for _ in range(7)]
    dma = pltpu.SemaphoreType.DMA
    scratch += [dma((7,)), dma((24,)), dma((24,)), dma((3, no)), dma((3, no))]
    air, sea = pl.pallas_call(
        functools.partial(kernel, na, no, cap),
        out_shape=(
            jax.ShapeDtypeStruct((2 * LEV * ROWS, W), f32),
            jax.ShapeDtypeStruct((16, BLK, W), f32),
        ),
        in_specs=[hbm, hbm, hbm, vmem, vmem, vmem, vmem, hbm, hbm, smem, vmem, vmem, vmem, smem],
        out_specs=(hbm, hbm),
        scratch_shapes=scratch,
        compiler_params=pltpu.CompilerParams(
            collective_id=0, has_side_effects=True, vmem_limit_bytes=63 * 1024 * 1024
        ),
    )(
        atm_state.reshape(2 * LEV, ROWS, W),
        atm_state.reshape(2 * LEV * ROWS, W),
        ocn_state.reshape(16, BLK, W),
        land,
        ocn_kappa,
        partner.reshape(1, BLK),
        partner_row.reshape(1, BLK),
        remap_up,
        remap_down,
        surface_mix,
        drag,
        level_kappa.reshape(1, LEV),
        vertical_mix,
        depth_gain.reshape(1, 4),
    )
    return air.reshape(atm_state.shape), sea.reshape(ocn_state.shape)


def solution(mesh):
    placed = (
        P(None, None, "atm", "ocn"),
        P(None, None, "atm", "ocn"),
        P("atm", "ocn"),
        P("atm", "ocn"),
        P("ocn", "atm", None),
        P("ocn", "atm", None),
        P("atm", "ocn", None),
        P("atm", "ocn", None),
        P(),
        P("atm", "ocn"),
        P(),
        P(),
        P(),
    )
    return jax.shard_map(
        functools.partial(shards, mesh.shape["atm"], mesh.shape["ocn"]),
        mesh=mesh,
        in_specs=placed,
        out_specs=(P(None, None, "atm", "ocn"), P(None, None, "atm", "ocn")),
        check_vma=False,
    )
```

profile of v0, /device:TPU:1, one launch (start us, length us, event | category | flops | bytes accessed | tf_op | source)
XLA Modules:
  0.0 89.5 jit_solution(4847318965607812799)
XLA Ops:
  0.6 84.7 %shard_map.140 = (f32[4608,128]{1,0:T(8,128)}, f32[16,64,128]{2,1,0:T(8,128)}) custom-call(f32[144,32,128]{2,1,0:T(8,128)} %bitcast.9, f32[4608,128]{1,0:T(8,128)} %bitcast.10, f32[16,64,128]{2,1,0:T(8,128)} %bitcast.12, s32[64,128]{1,0:T(8,128)} %land.1, f32[64,128]{1,0:T(8,128)} %kappa.1, s32[1,64]{1,0:T(1,128)} %bitcast.14, s32[1,64]{1,0:T(1,128)} %bitcast.15, ...), custom_call_target="tpu_custom_call" | custom-call | tf_op jit(solution)/shard_map/pallas_call | solution.py:590
  85.4 0.0 copy-start
  85.4 3.3 %copy.17 = f32[2,72,32,128]{3,2,1,0:T(8,128)} copy(f32[2,72,32,128]{3,2,1,0:T(8,128)} %bitcast.11) | data formatting | bytes 4718592
  88.7 0.0 copy-done
  88.7 0.8 copy.18
Async XLA Ops:
  85.4 3.3 %copy-start = (f32[16,64,128]{2,1,0:T(8,128)S(1)}, f32[16,64,128]{2,1,0:T(8,128)}, u32[]{:S(2)}) copy-start(f32[16,64,128]{2,1,0:T(8,128)} %get-tuple-element.5) | copy-start | bytes 1572868
where the time goes:
time: 89.8 us; the launch traced here: 89.5 us
  Pallas kernels  84.7 us (94%)
  local copies, waits for them, and re-layouts  4.13 us (5%)
    pallas_call x1, Pallas kernels, shards(): pl.pallas_call(functools.partial(kernel, na, no, cap), out_shape=(jax.Sha...  84.7 us
    unnamed x4, local copies, waits for them, and re-layouts  4.13 us

commit v1 on v0

--- a/solution.py
+++ b/solution.py
@@ -2,6 +2,7 @@
 
 import jax
 import jax.numpy as jnp
+import numpy as np
 from jax import lax
 from jax.experimental import pallas as pl
 from jax.experimental.pallas import tpu as pltpu
@@ -52,12 +53,67 @@
     return pltpu.roll(x, shift, axis)
 
 
+SEG = 3 * ASTEPS
+OWN = 2 * ASTEPS
+
+
+def sines(n):
+    k = np.arange(1, n + 1)
+    return np.sqrt(2.0 / (n + 1)) * np.sin(np.pi * np.outer(k, k) / (n + 1)), 2.0 * np.cos(np.pi * k / (n + 1))
+
+
+def two_parts(m):
+    hi = np.asarray(m, np.float32).astype(jnp.bfloat16)
+    mid = (np.asarray(m, np.float64) - hi.astype(np.float64)).astype(np.float32).astype(jnp.bfloat16)
+    return hi, mid
+
+
+def wide_parts(m):
+    hi, mid = two_parts(m)
+    return np.concatenate([np.concatenate([hi, mid], 1), np.concatenate([hi, np.zeros_like(mid)], 1)], 0)
+
+
+def transforms():
+    q, d = sines(W)
+    back = q.copy()
+    back[:, :ASTEPS] = 0.0
+    back[:, W - ASTEPS:] = 0.0
+    gf, gi, ds = [], [], []
+    for kind in range(3):
+        there, again, eig = np.zeros((W, W)), np.zeros((W, 2 * W)), np.zeros((1, W))
+        for seg in range(4):
+            var, side = divmod(seg, 2)
+            places = list(range(SEG))
+            if kind == 1 and side == 0:
+                places = places[ASTEPS:]
+            if kind == 2 and side == 1:
+                places = places[:OWN]
+            basis, values = sines(len(places))
+            for n, place in enumerate(places):
+                col = place - ASTEPS if side == 0 else W - OWN + place
+                if col < 0:
+                    lane = 64 + 24 * var + col + ASTEPS
+                elif col >= W:
+                    lane = 70 + 24 * var + col - W
+                else:
+                    lane = (col + 24 * var) % W
+                there[lane, SEG * seg:SEG * seg + len(places)] = basis[n]
+                if ASTEPS <= place < OWN:
+                    again[SEG * seg:SEG * seg + len(places), W * var + col] = basis[:, n]
+            eig[0, SEG * seg:SEG * seg + len(places)] = values
+        gf.append(wide_parts(there))
+        hi, mid = two_parts(again)
+        gi.append(np.concatenate([hi, hi, mid], 0))
+        ds.append(np.concatenate([d.reshape(1, W), eig] + [np.zeros((1, W))] * 6, 0))
+    return wide_parts(q), wide_parts(back), np.stack(gf), np.stack(gi), np.stack(ds).astype(np.float32)
+
+
 def kernel(
     na, no, cap,
-    atm, atm_flat, ocn, land, kappa, partner, prow, up, down, smix, drag, lk, vm, gain,
+    atm, atm_flat, ocn, land, kappa, partner, prow, up, down, smix, drag, lk, vm, gain, qf, qi, gf, gi, eig,
     atm_out, ocn_out,
     a_flat, a_top, a_bot, top_flat, bot_flat, u_own, up_v, down_v,
-    r_out, l_out, d_out, l_in, r_in, d_in,
+    own_e, e_out, l_in, r_in, d_in,
     ob, oe, ob_top, ob_bot, oe_l, oe_r, oe_c,
     rid_out, rid_in, c_out, c_in, p_out, p_in,
     fx, fx_l, fx_r, fx_t, fx_b, fx_c,
@@ -201,29 +257,25 @@
     def own_row(v, x):
         return a_flat[pl.ds(v * LEV * ROWS + x, LEV, stride=ROWS), :]
 
-    for half in range(2):
-        for v in range(2):
-            def gather(i, carry):
-                to_r, to_l = carry
-                row = own_row(v, half * 16 + i)
-                here = lane // 8 == i
-                return (
-                    jnp.where(here, rolled(row, lax.rem(8 * i + 6, W)), to_r),
-                    jnp.where(here, rolled(row, 8 * i), to_l),
-                )
-            to_r, to_l = lax.fori_loop(0, 16, gather, (jnp.zeros((LEV, W), f32), jnp.zeros((LEV, W), f32)))
-            r_out[half, v] = to_r
-            l_out[half, v] = to_l
-    for n, buf in ((0, r_out), (2, l_out)):
-        d_out[n] = jnp.where(lane < 64, buf[0, 0], rolled(buf[0, 1], 64))
-        d_out[n + 1] = jnp.where(lane < 64, rolled(buf[1, 0], 64), buf[1, 1])
+    def gather(g, xs):
+        packed = jnp.zeros((LEV, W), f32)
+        for n, x in enumerate(xs):
+            if x is not None:
+                e = jnp.where((lane >= OWN) & (lane < 3 * OWN), rolled(own_row(1, x), 2 * OWN), own_row(0, x))
+                own_e[x] = e
+                packed = jnp.where((lane >= 42 * n) & (lane < 42 * n + 42), rolled(e, 42 * n + 6), packed)
+        e_out[g] = packed
+
+    lax.fori_loop(0, 5, lambda g, _: (gather(g, [3 * g + n for n in range(3)]), 0)[1], 0)
+    gather(5, [15, None, 16])
+    lax.fori_loop(6, 11, lambda g, _: (gather(g, [3 * g + n - 1 for n in range(3)]), 0)[1], 0)
     h_e = [
-        send(r_out, l_in, 10, me_a, right),
-        send(l_out, r_in, 11, me_a, left),
-        send(d_out.at[1], d_in.at[0], 12, below, right),
-        send(d_out.at[3], d_in.at[1], 13, below, left),
-        send(d_out.at[0], d_in.at[2], 14, above, right),
-        send(d_out.at[2], d_in.at[3], 15, above, left),
+        send(e_out, l_in, 10, me_a, right),
+        send(e_out, r_in, 11, me_a, left),
+        send(e_out.at[pl.ds(9, 2)], d_in.at[0], 12, below, right),
+        send(e_out.at[pl.ds(9, 2)], d_in.at[1], 13, below, left),
+        send(e_out.at[pl.ds(0, 2)], d_in.at[2], 14, above, right),
+        send(e_out.at[pl.ds(0, 2)], d_in.at[3], 15, above, left),
     ]
 
     exact = lax.Precision.HIGHEST
@@ -260,23 +312,35 @@
     wf = chi + rolled(chi, 8) + rolled(column - chi, 16)
     wf_s[...] = jnp.concatenate([wf, jnp.zeros((8, W), f32)], 0)[:, :32].astype(bf16)
 
-    def powers(x):
+    def parts2(x):
+        hi = x.astype(bf16)
+        return hi, (x - hi.astype(f32)).astype(bf16)
+
+    def changed(rows, matrix):
+        res = mm(jnp.concatenate(parts2(jnp.concatenate(rows, 0)), 1), matrix)
+        res = res[:, :W] + res[:, W:]
+        return [res[LEV * n:LEV * (n + 1)] for n in range(len(rows))]
+
+    def powers(x, low=0):
         hi = high(x)
         z = jnp.zeros((8, 2 * W), f32)
         h = jnp.concatenate([hi, z], 0).astype(bf16)
         m = jnp.concatenate([x - hi, z], 0).astype(bf16)
-        return mm(w_s[...], jnp.concatenate([h, m, h], 0))
-
-    def put_row(r, x):
-        res = powers(x)
-        for k in range(7):
-            pm[k][r] = res[LEV * k:LEV * (k + 1)]
-
-    def own_body(x, _):
-        put_row(x + ASTEPS, jnp.concatenate([own_row(0, x), own_row(1, x)], 1))
+        return mm(w_s[pl.ds(LEV * low, 512 - LEV * low), :], jnp.concatenate([h, m, h], 0))
+
+    def put(refs, places, rows, matrix, low=0):
+        turned = changed(rows, matrix)
+        for n, place in enumerate(places):
+            res = powers(jnp.concatenate(turned[2 * n:2 * n + 2], 1), low)
+            for k in range(low, 7):
+                refs[k][place] = res[LEV * (k - low):LEV * (k - low + 1)]
+
+    def own_body(i, _):
+        xs = [4 * i + n for n in range(4)]
+        put(pm, [x + ASTEPS for x in xs], [own_row(v, x) for x in xs for v in range(2)], qf[...])
         return 0
 
-    lax.fori_loop(0, ROWS // 2, own_body, 0, unroll=2)
+    lax.fori_loop(0, ROWS // 8, own_body, 0)
 
     rid_in[mine_rows] = rid_out[mine_rows]
     c_in[mine_rows] = c_out[mine_rows]
@@ -303,7 +367,7 @@
         send(fx.at[:, pl.ds(0, 8)], fx_c.at[3], 23, above, left),
     ]
 
-    lax.fori_loop(ROWS // 2, ROWS, own_body, 0, unroll=2)
+    lax.fori_loop(ROWS // 8, ROWS // 4, own_body, 0)
 
     h_top.wait_recv()
     h_bot.wait_recv()
@@ -314,84 +378,50 @@
     def beside_row(flat, v, x):
         return flat[pl.ds(v * LEV * 8 + x, LEV, stride=8), :]
 
-    def beside_body(x, _):
-        put_row(x, jnp.concatenate([beside_row(top_flat, 0, x + 2), beside_row(top_flat, 1, x + 2)], 1))
-        put_row(x + ROWS + ASTEPS, jnp.concatenate([beside_row(bot_flat, 0, x), beside_row(bot_flat, 1, x)], 1))
+    for r in range(ASTEPS):
+        put(
+            pm, [r, EXT - 1 - r],
+            [beside_row(top_flat, v, r + 2) for v in range(2)]
+            + [beside_row(bot_flat, v, ASTEPS - 1 - r) for v in range(2)],
+            qf[...], (ASTEPS - r) // 2 * 2,
+        )
+
+    arrive(h_e)
+    kind = jnp.where(me_o == 0, 1, jnp.where(me_o == no - 1, 2, 0))
+    spot = lax.rem(lane, 42)
+    from_left = (spot < 6) | ((spot >= 24) & (spot < 30))
+
+    def strip(e, lefts, rights, n):
+        shift = 64 - 42 * n if isinstance(n, int) else lax.rem(64 + W - 42 * n, W)
+        beside = rolled(jnp.where(from_left, lefts, rights), shift)
+        return jnp.where((lane >= 64) & (lane < 106), beside, e)
+
+    def strip_body(i, _):
+        made = []
+        for h in range(4):
+            x = 4 * i + h
+            at = x + jnp.where(i >= 4, 1, 0)
+            g = lax.div(at, 3)
+            made.append(strip(own_e[x], l_in[g], r_in[g], at - 3 * g))
+        put(sm, [2 * i + ASTEPS // 2 + 1, 2 * i + ASTEPS // 2 + 2], made, gf[kind])
         return 0
 
-    lax.fori_loop(0, ASTEPS, beside_body, 0)
-
-    arrive(h_e)
-
-    @pl.when(me_o == 0)
-    def _():
-        l_in[...] = jnp.zeros_like(l_in)
-        d_in[0] = jnp.zeros((LEV, W), f32)
-        d_in[2] = jnp.zeros((LEV, W), f32)
-
-    @pl.when(me_o == no - 1)
-    def _():
-        r_in[...] = jnp.zeros_like(r_in)
-        d_in[1] = jnp.zeros((LEV, W), f32)
-        d_in[3] = jnp.zeros((LEV, W), f32)
-
-    @pl.when(me_a == 0)
-    def _():
-        d_in[0] = jnp.zeros((LEV, W), f32)
-        d_in[1] = jnp.zeros((LEV, W), f32)
-
-    @pl.when(me_a == na - 1)
-    def _():
-        d_in[2] = jnp.zeros((LEV, W), f32)
-        d_in[3] = jnp.zeros((LEV, W), f32)
-
-    def strip(own0, own1, lefts, rights, place0, place1):
-        out = jnp.where(lane < 12, own0, rolled(own0, 64))
-        out = jnp.where(lane >= 122, rolled(lefts[0], lax.rem(122 + W - place0, W)), out)
-        out = jnp.where((lane >= 64) & (lane < 70), rolled(rights[0], lax.rem(64 + W - place0, W)), out)
-        out = jnp.where((lane >= 32) & (lane < 44), rolled(own1, 32), out)
-        out = jnp.where((lane >= 84) & (lane < 96), rolled(own1, 96), out)
-        out = jnp.where((lane >= 26) & (lane < 32), rolled(lefts[1], lax.rem(26 + W - place1, W)), out)
-        return jnp.where((lane >= 96) & (lane < 102), rolled(rights[1], lax.rem(96 + W - place1, W)), out)
-
-    def put_pair(pair, x):
-        res = powers(x)
-        for k in range(7):
-            sm[k][pair + 1] = res[LEV * k:LEV * (k + 1)]
-
-    for half in range(2):
-        def strip_body(i, _):
-            made = []
+    lax.fori_loop(0, ROWS // 4, strip_body, 0)
+    for q in range(ASTEPS // 2):
+        made = []
+        for flat, first, corner, there in ((top_flat, 2, 0, me_a > 0), (bot_flat, 0, 2, me_a < na - 1)):
             for h in range(2):
-                n = 2 * i + h
-                x = half * 16 + n
-                made.append(strip(
-                    own_row(0, x), own_row(1, x),
-                    (l_in[half, 0], l_in[half, 1]), (r_in[half, 0], r_in[half, 1]), 8 * n, 8 * n,
-                ))
-            put_pair(half * 8 + i + ASTEPS // 2, jnp.concatenate(made, 1))
-            return 0
-        lax.fori_loop(0, 8, strip_body, 0)
-    for flat, first, base, corner in ((top_flat, 2, 0, 0), (bot_flat, 0, (ROWS + ASTEPS) // 2, 2)):
-        def corner_body(i, _):
-            made = []
-            for h in range(2):
-                x = 2 * i + h + first
-                made.append(strip(
-                    beside_row(flat, 0, x), beside_row(flat, 1, x),
-                    (d_in[corner], d_in[corner]), (d_in[corner + 1], d_in[corner + 1]), 8 * x, 8 * x + 64,
-                ))
-            put_pair(base + i, jnp.concatenate(made, 1))
-            return 0
-        lax.fori_loop(0, ASTEPS // 2, corner_body, 0)
-    for k in range(7):
-        sm[k][0] = jnp.zeros((LEV, 2 * W), f32)
-        sm[k][PAIRS + 1] = jnp.zeros((LEV, 2 * W), f32)
-
-    lane1 = lanes((1, W))
-    outside_l = ((lane1 >= 122) | ((lane1 >= 26) & (lane1 < 32))) & (me_o == 0)
-    outside_r = (((lane1 >= 64) & (lane1 < 70)) | ((lane1 >= 96) & (lane1 < 102))) & (me_o == no - 1)
-    inside = jnp.where(outside_l | outside_r, 0.0, 1.0)
+                r = 2 * q + h if corner == 0 else ASTEPS - 2 - 2 * q + h
+                e0, e1 = beside_row(flat, 0, r + first), beside_row(flat, 1, r + first)
+                e = jnp.where((lane >= OWN) & (lane < 3 * OWN), rolled(e1, 2 * OWN), e0)
+                z = strip(e, d_in[corner, r // 3], d_in[corner + 1, r // 3], r % 3)
+                made.append(jnp.where(there, z, 0.0))
+        put(sm, [q + 1, PAIRS - q], made, gf[kind], (ASTEPS - 2 * q - 1) // 2 * 2)
+    s6[0] = jnp.zeros((LEV, 2 * W), f32)
+    s6[PAIRS + 1] = jnp.zeros((LEV, 2 * W), f32)
+
+    d_main = jnp.broadcast_to(eig[0, pl.ds(0, 1), :], (LEV, W))
+    d_strip = jnp.broadcast_to(eig[kind, pl.ds(1, 1), :], (LEV, W))
 
     for k in range(ASTEPS - 1, -1, -1):
         src, dst = pm[k + 1], pm[k]
@@ -407,7 +437,7 @@
                 made = []
                 for n in range(group):
                     c = near[n + 1]
-                    made.append(dst[r + n, :, sl] + ((near[n] + near[n + 2]) + (rolled(c, 1) + rolled(c, W - 1))))
+                    made.append(dst[r + n, :, sl] + ((near[n] + near[n + 2]) + d_main * c))
                 for n in range(group):
                     dst[r + n, :, sl] = made[n]
             return 0
@@ -418,10 +448,8 @@
         def strip_step(i, _):
             q = i + first // 2
             a0, a1 = ssrc[q + 1, :, :W], ssrc[q + 1, :, W:]
-            made0 = (ssrc[q, :, W:] + a1) + (rolled(a0, 1) + rolled(a0, W - 1))
-            made1 = (ssrc[q + 2, :, :W] + a0) + (rolled(a1, 1) + rolled(a1, W - 1))
-            sdst[q + 1, :, :W] = sdst[q + 1, :, :W] + made0 * inside
-            sdst[q + 1, :, W:] = sdst[q + 1, :, W:] + made1 * inside
+            sdst[q + 1, :, :W] = sdst[q + 1, :, :W] + ((ssrc[q, :, W:] + a1) + d_strip * a0)
+            sdst[q + 1, :, W:] = sdst[q + 1, :, W:] + ((ssrc[q + 2, :, :W] + a0) + d_strip * a1)
             return 0
         lax.fori_loop(0, PAIRS - 2 * (first // 2), strip_step, 0)
 
@@ -537,19 +565,20 @@
                 )
 
     def final_body(i, _):
+        mids = [p0[2 * i + h + ASTEPS, :, W * v:W * (v + 1)] for h in range(2) for v in range(2)]
+        mids = changed(mids, qi[...])
+        e = s0[i + ASTEPS // 2 + 1]
+        hi, mid = parts2(jnp.concatenate([e[:, :W], e[:, W:]], 0))
+        side = mm(jnp.concatenate([hi, mid, hi], 1), gi[kind])
         for h in range(2):
             x = 2 * i + h
             at = pl.ds(pl.multiple_of(8 * x, 8), 8)
             g = jnp.concatenate([gs[0, at, :], gs[1, at, :]], 1)
             hi = high(g)
             rhs = jnp.concatenate([hi, g - hi, hi, jnp.zeros((8, 2 * W), f32)], 0).astype(bf16)
-            extra = mm(wf_s[...], rhs)[:LEV]
-            e = s0[i + ASTEPS // 2 + 1, :, W * h:W * (h + 1)]
+            extra = mm(wf_s[...], rhs)[:LEV] + side[LEV * h:LEV * (h + 1)]
             for v in range(2):
-                res = p0[x + ASTEPS, :, W * v:W * (v + 1)]
-                res = jnp.where(lane < 6, rolled(e, -32 * v), res)
-                res = jnp.where(lane >= 122, rolled(e, 64 - 32 * v), res)
-                out_a[pl.ds(v * LEV * ROWS + x, LEV, stride=ROWS), :] = res + extra[:, W * v:W * (v + 1)]
+                out_a[pl.ds(v * LEV * ROWS + x, LEV, stride=ROWS), :] = mids[2 * h + v] + extra[:, W * v:W * (v + 1)]
         return 0
 
     lax.fori_loop(0, ROWS // 2, final_body, 0)
@@ -576,7 +605,7 @@
 
     scratch = [
         v(2 * LEV * ROWS, W), v(2 * LEV, 8, W), v(2 * LEV, 8, W), v(2 * LEV * 8, W), v(2 * LEV * 8, W), v(16, BLK, W), v(BLK, W, W), v(BLK, W, W),
-        v(2, 2, LEV, W), v(2, 2, LEV, W), v(4, LEV, W), v(2, 2, LEV, W), v(2, 2, LEV, W), v(4, LEV, W),
+        v(ROWS, LEV, W), v(11, LEV, W), v(11, LEV, W), v(11, LEV, W), v(4, 2, LEV, W),
         v(18, BLK, W), v(2, BLK, W), v(18, 8, W), v(18, 8, W), v(2, BLK, W), v(2, BLK, W), v(4, 2, 8, W),
         v(slots, W), v(slots, W), v(slots, 4 * W), v(slots, 4 * W), v(slots, 4 * W), v(slots, 4 * W),
         v(2, ROWS, W), v(2, ROWS, W), v(2, ROWS, W), v(2, 8, W), v(2, 8, W), v(4, 2, 8, W),
@@ -593,7 +622,7 @@
             jax.ShapeDtypeStruct((2 * LEV * ROWS, W), f32),
             jax.ShapeDtypeStruct((16, BLK, W), f32),
         ),
-        in_specs=[hbm, hbm, hbm, vmem, vmem, vmem, vmem, hbm, hbm, smem, vmem, vmem, vmem, smem],
+        in_specs=[hbm, hbm, hbm, vmem, vmem, vmem, vmem, hbm, hbm, smem, vmem, vmem, vmem, smem] + [vmem] * 5,
         out_specs=(hbm, hbm),
         scratch_shapes=scratch,
         compiler_params=pltpu.CompilerParams(
@@ -614,6 +643,7 @@
         level_kappa.reshape(1, LEV),
         vertical_mix,
         depth_gain.reshape(1, 4),
+        *[jnp.asarray(m) for m in transforms()],
     )
     return air.reshape(atm_state.shape), sea.reshape(ocn_state.shape)
 

time: 89.8 us -> 68.4 us (0.76)
  Pallas kernels: 84.7 us -> 63.4 us
    pallas_call x1, Pallas kernels: 84.7 us -> 63.4 us  [shards(): pl.pallas_call(functools.partial(kernel, na, no, cap), out_shape=(jax.Sha...]
where the time goes in v1:
time: 68.4 us; the launch traced here: 68.2 us
  Pallas kernels  63.4 us (93%)
  local copies, waits for them, and re-layouts  4.13 us (6%)
    pallas_call x1, Pallas kernels, shards(): pl.pallas_call(functools.partial(kernel, na, no, cap), out_shape=(jax.Sha...  63.4 us
    unnamed x4, local copies, waits for them, and re-layouts  4.13 us

profile of v1, /device:TPU:1, one launch (start us, length us, event | category | flops | bytes accessed | tf_op | source)
XLA Modules:
  0.0 68.2 jit_solution(16044839746080088025)
XLA Ops:
  0.6 63.4 %shard_map.185 = (f32[4608,128]{1,0:T(8,128)}, f32[16,64,128]{2,1,0:T(8,128)}) custom-call(f32[144,32,128]{2,1,0:T(8,128)} %bitcast.9, f32[4608,128]{1,0:T(8,128)} %bitcast.10, f32[16,64,128]{2,1,0:T(8,128)} %bitcast.12, s32[64,128]{1,0:T(8,128)} %land.1, f32[64,128]{1,0:T(8,128)} %kappa.1, s32[1,64]{1,0:T(1,128)} %bitcast.14, s32[1,64]{1,0:T(1,128)} %bitcast.15, ...), custom_call_target="tpu_custom_call" | custom-call | tf_op jit(solution)/shard_map/pallas_call | solution.py:619
  64.1 0.0 copy-start
  64.1 3.3 %copy.22 = f32[2,72,32,128]{3,2,1,0:T(8,128)} copy(f32[2,72,32,128]{3,2,1,0:T(8,128)} %bitcast.11) | data formatting | bytes 4718592
  67.4 0.0 copy-done
  67.4 0.8 %copy.23 = f32[4,4,64,128]{3,2,1,0:T(8,128)} copy(f32[4,4,64,128]{3,2,1,0:T(8,128)S(1)} %bitcast.13) | data formatting | bytes 1048576
Async XLA Ops:
  64.1 3.3 %copy-start = (f32[16,64,128]{2,1,0:T(8,128)S(1)}, f32[16,64,128]{2,1,0:T(8,128)}, u32[]{:S(2)}) copy-start(f32[16,64,128]{2,1,0:T(8,128)} %get-tuple-element.5) | copy-start | bytes 1572868

commit v2 on v1

--- a/solution.py
+++ b/solution.py
@@ -113,7 +113,7 @@
     atm, atm_flat, ocn, land, kappa, partner, prow, up, down, smix, drag, lk, vm, gain, qf, qi, gf, gi, eig,
     atm_out, ocn_out,
     a_flat, a_top, a_bot, top_flat, bot_flat, u_own, up_v, down_v,
-    own_e, e_out, l_in, r_in, d_in,
+    own_e, r_out, l_out, l_in, r_in, d_in,
     ob, oe, ob_top, ob_bot, oe_l, oe_r, oe_c,
     rid_out, rid_in, c_out, c_in, p_out, p_in,
     fx, fx_l, fx_r, fx_t, fx_b, fx_c,
@@ -181,55 +181,8 @@
 
     mine_rows = pl.ds(pl.multiple_of(me_o * cap, 8), cap)
 
-    h_bot = send(atm.at[:, pl.ds(0, 8)], a_bot, 0, above, me_o)
-    h_top = send(atm.at[:, pl.ds(ROWS - 8, 8)], a_top, 1, below, me_o)
-
-    t_row = partner[...].astype(f32)
-    r_row = prow[...].astype(f32)
-    ii, jj = rows_of((BLK, BLK)), lanes((BLK, BLK))
-    t_all = jnp.broadcast_to(t_row, (BLK, BLK))
-    t_col = jnp.sum(jnp.where(ii == jj, t_all, 0.0), axis=1, keepdims=True)
-    same = t_col == t_all
-    pos_row = jnp.sum(jnp.where(same & (ii < jj), 1.0, 0.0), axis=0, keepdims=True)
-    pos_col = jnp.sum(jnp.where(same & (jj < ii), 1.0, 0.0), axis=1, keepdims=True)
-    slot_row = t_row * cap + pos_row
-    slot_col = t_col * cap + pos_col
-    chosen = jnp.where(rows_of((slots, BLK)).astype(f32) == slot_row, 1.0, 0.0)
-    chosen_t = jnp.where(lanes((BLK, slots)).astype(f32) == slot_col, 1.0, 0.0)
-    rid = jnp.sum(chosen * (r_row + 1.0), axis=1, keepdims=True) - 1.0
-    rid_out[...] = jnp.broadcast_to(rid, (slots, W))
-    g_rid = spread(rid_out, rid_in, 0)
-
     lf = land[...].astype(f32)
     g_ocn.wait()
-    for k in range(4):
-        total = smix[k, 0] * u_own[0]
-        for c in range(1, 16):
-            total = total + smix[k, c] * u_own[c]
-        total = total * lf
-        hi = high(total)
-        mx[pl.ds(k, BLK, stride=8), :] = hi
-        mx[pl.ds(4 + k, BLK, stride=8), :] = total - hi
-
-    def remap(b, weights, transposed):
-        block = weights[b]
-        hi = high(block)
-        parts = (hi.astype(bf16), (block - hi).astype(bf16))
-        vec = mx[pl.ds(pl.multiple_of(b * 8, 8), 8), :].astype(bf16)
-        if transposed:
-            res = mm(vec, jnp.concatenate(parts, 0), ((1,), (1,)))
-        else:
-            res = mm(vec, jnp.concatenate(parts, 1))
-        first = res[:, :W]
-        cb[pl.ds(pl.multiple_of(b * 8, 8), 8), :] = first + rolled(first, 4, 0) + res[:, W:]
-
-    for i in range(chunks):
-        g_up[i].wait()
-        lax.fori_loop(i * part, (i + 1) * part, lambda b, _: (remap(b, up_v, False), 0)[1], 0, unroll=4)
-    fields = jnp.concatenate([cb[pl.ds(k, BLK, stride=8), :] for k in range(4)], 1)
-    c_out[...] = pick(chosen, fields)
-    g_c = spread(c_out, c_in, 1)
-
     for c in range(16):
         ob[c] = u_own[c]
     ob[16] = lf
@@ -251,31 +204,81 @@
         send(oe.at[:, pl.ds(0, 8)], oe_c.at[3], 9, above, left),
     ]
 
+    h_bot = send(atm.at[:, pl.ds(0, 8)], a_bot, 0, above, me_o)
+    h_top = send(atm.at[:, pl.ds(ROWS - 8, 8)], a_top, 1, below, me_o)
+
+    t_row = partner[...].astype(f32)
+    r_row = prow[...].astype(f32)
+    ii, jj = rows_of((BLK, BLK)), lanes((BLK, BLK))
+    t_all = jnp.broadcast_to(t_row, (BLK, BLK))
+    t_col = jnp.sum(jnp.where(ii == jj, t_all, 0.0), axis=1, keepdims=True)
+    same = t_col == t_all
+    pos_row = jnp.sum(jnp.where(same & (ii < jj), 1.0, 0.0), axis=0, keepdims=True)
+    pos_col = jnp.sum(jnp.where(same & (jj < ii), 1.0, 0.0), axis=1, keepdims=True)
+    slot_row = t_row * cap + pos_row
+    slot_col = t_col * cap + pos_col
+    chosen = jnp.where(rows_of((slots, BLK)).astype(f32) == slot_row, 1.0, 0.0)
+    chosen_t = jnp.where(lanes((BLK, slots)).astype(f32) == slot_col, 1.0, 0.0)
+    rid = jnp.sum(chosen * (r_row + 1.0), axis=1, keepdims=True) - 1.0
+    rid_out[...] = jnp.broadcast_to(rid, (slots, W))
+    g_rid = spread(rid_out, rid_in, 0)
+
+    for k in range(4):
+        total = smix[k, 0] * u_own[0]
+        for c in range(1, 16):
+            total = total + smix[k, c] * u_own[c]
+        total = total * lf
+        hi = high(total)
+        mx[pl.ds(k, BLK, stride=8), :] = hi
+        mx[pl.ds(4 + k, BLK, stride=8), :] = total - hi
+
+    def remap(b, weights, transposed):
+        block = weights[b]
+        hi = high(block)
+        parts = (hi.astype(bf16), (block - hi).astype(bf16))
+        vec = mx[pl.ds(pl.multiple_of(b * 8, 8), 8), :].astype(bf16)
+        if transposed:
+            res = mm(vec, jnp.concatenate(parts, 0), ((1,), (1,)))
+        else:
+            res = mm(vec, jnp.concatenate(parts, 1))
+        first = res[:, :W]
+        cb[pl.ds(pl.multiple_of(b * 8, 8), 8), :] = first + rolled(first, 4, 0) + res[:, W:]
+
+    for i in range(chunks):
+        g_up[i].wait()
+        lax.fori_loop(i * part, (i + 1) * part, lambda b, _: (remap(b, up_v, False), 0)[1], 0, unroll=4)
+    fields = jnp.concatenate([cb[pl.ds(k, BLK, stride=8), :] for k in range(4)], 1)
+    c_out[...] = pick(chosen, fields)
+    g_c = spread(c_out, c_in, 1)
+
     g_atm.wait()
     lane = lanes((LEV, W))
 
     def own_row(v, x):
         return a_flat[pl.ds(v * LEV * ROWS + x, LEV, stride=ROWS), :]
 
-    def gather(g, xs):
-        packed = jnp.zeros((LEV, W), f32)
-        for n, x in enumerate(xs):
-            if x is not None:
-                e = jnp.where((lane >= OWN) & (lane < 3 * OWN), rolled(own_row(1, x), 2 * OWN), own_row(0, x))
-                own_e[x] = e
-                packed = jnp.where((lane >= 42 * n) & (lane < 42 * n + 42), rolled(e, 42 * n + 6), packed)
-        e_out[g] = packed
-
-    lax.fori_loop(0, 5, lambda g, _: (gather(g, [3 * g + n for n in range(3)]), 0)[1], 0)
-    gather(5, [15, None, 16])
-    lax.fori_loop(6, 11, lambda g, _: (gather(g, [3 * g + n - 1 for n in range(3)]), 0)[1], 0)
+    def gather(g, _):
+        to_r = to_l = jnp.zeros((LEV, W), f32)
+        for n in range(8):
+            x = 8 * g + n
+            e = jnp.where((lane >= OWN) & (lane < 3 * OWN), rolled(own_row(1, x), 2 * OWN), own_row(0, x))
+            own_e[x] = e
+            place = 6 * (n % 4) + 48 * (n // 4)
+            here = (lane // 48 == n // 4) & (lax.rem(lane, 24) // 6 == n % 4)
+            to_r = jnp.where(here, rolled(e, place + 6), to_r)
+            to_l = jnp.where(here, rolled(e, place), to_l)
+        r_out[g] = to_r
+        l_out[g] = to_l
+        return 0
+
+    lax.fori_loop(0, ROWS // 8, gather, 0)
     h_e = [
-        send(e_out, l_in, 10, me_a, right),
-        send(e_out, r_in, 11, me_a, left),
-        send(e_out.at[pl.ds(9, 2)], d_in.at[0], 12, below, right),
-        send(e_out.at[pl.ds(9, 2)], d_in.at[1], 13, below, left),
-        send(e_out.at[pl.ds(0, 2)], d_in.at[2], 14, above, right),
-        send(e_out.at[pl.ds(0, 2)], d_in.at[3], 15, above, left),
+        send(r_out, l_in, 10, me_a, right),
+        send(l_out, r_in, 11, me_a, left),
+        send(r_out.at[3], d_in.at[0], 12, below, right),
+        send(l_out.at[3], d_in.at[1], 13, below, left),
+        send(r_out.at[0], d_in.at[2], 14, above, right),
+        send(l_out.at[0], d_in.at[3], 15, above, left),
     ]
 
     exact = lax.Precision.HIGHEST
@@ -335,12 +338,73 @@
             for k in range(low, 7):
                 refs[k][place] = res[LEV * (k - low):LEV * (k - low + 1)]
 
+    arrive(h_ob)
+    tall = BLK + 16
+    rr = rows_of((tall, W))
+    row_in = ((rr >= 8) | (me_a > 0)) & ((rr < BLK + 8) | (me_a < na - 1))
+    lane_t = lanes((tall, W))
+
+    def tall_of(c):
+        return jnp.concatenate([ob_top[c], ob[c], ob_bot[c]], 0)
+
+    def tall_edge(n, side):
+        body = oe_l[n] if side == 0 else oe_r[n]
+        return jnp.concatenate([oe_c[side, n], body, oe_c[2 + side, n]], 0)
+
+    def neighbours(x):
+        return (rolled(x, 1, 0) + rolled(x, tall - 1, 0)) + (rolled(x, 1) + rolled(x, W - 1))
+
+    def stepped(x, c0, c1):
+        for _ in range(OSTEPS):
+            x = c0 * x + c1 * neighbours(x)
+        return x
+
+    sea = jnp.where(row_in, tall_of(16), 0.0)
+    kap = tall_of(17)
+    c1 = kap * sea
+    c0 = sea - c1 * neighbours(sea)
+
+    def edges(own, l_edge, r_edge, at, slot):
+        out = jnp.where(lane_t < 32 * slot + 4, rolled(l_edge, 32 * slot - at), rolled(own, 32 * slot + 4))
+        out = jnp.where(lane_t >= 32 * slot + 16, rolled(own, 32 * slot + 24), out)
+        return jnp.where(lane_t >= 32 * slot + 24, rolled(r_edge, 32 * slot + 20 - at), out)
+
+    in_l = (lane_t >= 4) | (me_o > 0)
+    in_r = (lane_t < 24) | (me_o < no - 1)
+    used = ((lane_t < 12) | ((lane_t >= 16) & (lane_t < 28))) & in_l & in_r & row_in
+    tl, tr = tall_edge(1, 0), tall_edge(1, 1)
+    e_sea = jnp.where(used, edges(tall_of(16), tl, tr, 0, 0), 0.0)
+    e_kap = jnp.where(used, edges(kap, tl, tr, 8, 0), 0.0)
+
+    def four(x):
+        return (x + rolled(x, 32)) + (rolled(x, 64) + rolled(x, 96))
+
+    e_sea, e_kap = four(e_sea), four(e_kap)
+    e1 = e_kap * e_sea
+    e0 = e_sea - e1 * neighbours(e_sea)
+    ul, ur = tall_edge(0, 0), tall_edge(0, 1)
+    for g in range(4):
+        total = edges(tall_of(4 * g), ul, ur, 32 * g, 0)
+        for s in range(1, 4):
+            c = 4 * g + s
+            total = jnp.where(lane_t >= 32 * s, edges(tall_of(c), ul, ur, 8 * c, s), total)
+        st[g] = stepped(e_sea * total, e0, e1)[8:8 + BLK]
+
+    def channel(c, e, slot):
+        mid = stepped(sea * tall_of(c), c0, c1)[8:8 + BLK]
+        mid = jnp.where(lane64 < 4, rolled(e, lax.rem(2 * W - 32 * slot - 4, W)), mid)
+        mid = jnp.where(lane64 >= W - 4, rolled(e, lax.rem(W + 104 - 32 * slot, W)), mid)
+        us[c] = mid + (1.0 - lf) * u_own[c]
+
     def own_body(i, _):
         xs = [4 * i + n for n in range(4)]
         put(pm, [x + ASTEPS for x in xs], [own_row(v, x) for x in xs for v in range(2)], qf[...])
+        for h in range(2):
+            slot = 2 * lax.rem(i, 2) + h
+            channel(2 * i + h, st[lax.div(i, 2)], slot)
         return 0
 
-    lax.fori_loop(0, ROWS // 8, own_body, 0)
+    lax.fori_loop(0, ROWS // 4, own_body, 0)
 
     rid_in[mine_rows] = rid_out[mine_rows]
     c_in[mine_rows] = c_out[mine_rows]
@@ -367,8 +431,6 @@
         send(fx.at[:, pl.ds(0, 8)], fx_c.at[3], 23, above, left),
     ]
 
-    lax.fori_loop(ROWS // 8, ROWS // 4, own_body, 0)
-
     h_top.wait_recv()
     h_bot.wait_recv()
 
@@ -386,43 +448,7 @@
             qf[...], (ASTEPS - r) // 2 * 2,
         )
 
-    arrive(h_e)
-    kind = jnp.where(me_o == 0, 1, jnp.where(me_o == no - 1, 2, 0))
-    spot = lax.rem(lane, 42)
-    from_left = (spot < 6) | ((spot >= 24) & (spot < 30))
-
-    def strip(e, lefts, rights, n):
-        shift = 64 - 42 * n if isinstance(n, int) else lax.rem(64 + W - 42 * n, W)
-        beside = rolled(jnp.where(from_left, lefts, rights), shift)
-        return jnp.where((lane >= 64) & (lane < 106), beside, e)
-
-    def strip_body(i, _):
-        made = []
-        for h in range(4):
-            x = 4 * i + h
-            at = x + jnp.where(i >= 4, 1, 0)
-            g = lax.div(at, 3)
-            made.append(strip(own_e[x], l_in[g], r_in[g], at - 3 * g))
-        put(sm, [2 * i + ASTEPS // 2 + 1, 2 * i + ASTEPS // 2 + 2], made, gf[kind])
-        return 0
-
-    lax.fori_loop(0, ROWS // 4, strip_body, 0)
-    for q in range(ASTEPS // 2):
-        made = []
-        for flat, first, corner, there in ((top_flat, 2, 0, me_a > 0), (bot_flat, 0, 2, me_a < na - 1)):
-            for h in range(2):
-                r = 2 * q + h if corner == 0 else ASTEPS - 2 - 2 * q + h
-                e0, e1 = beside_row(flat, 0, r + first), beside_row(flat, 1, r + first)
-                e = jnp.where((lane >= OWN) & (lane < 3 * OWN), rolled(e1, 2 * OWN), e0)
-                z = strip(e, d_in[corner, r // 3], d_in[corner + 1, r // 3], r % 3)
-                made.append(jnp.where(there, z, 0.0))
-        put(sm, [q + 1, PAIRS - q], made, gf[kind], (ASTEPS - 2 * q - 1) // 2 * 2)
-    s6[0] = jnp.zeros((LEV, 2 * W), f32)
-    s6[PAIRS + 1] = jnp.zeros((LEV, 2 * W), f32)
-
     d_main = jnp.broadcast_to(eig[0, pl.ds(0, 1), :], (LEV, W))
-    d_strip = jnp.broadcast_to(eig[kind, pl.ds(1, 1), :], (LEV, W))
-
     for k in range(ASTEPS - 1, -1, -1):
         src, dst = pm[k + 1], pm[k]
         first = ASTEPS - k
@@ -443,7 +469,54 @@
             return 0
         lax.fori_loop(0, count // group, main_body, 0)
 
+        if k:
+            @pl.when(me_a == 0)
+            def _():
+                for r in range(ASTEPS):
+                    dst[r] = jnp.zeros((LEV, 2 * W), f32)
+
+            @pl.when(me_a == na - 1)
+            def _():
+                for r in range(ASTEPS):
+                    dst[ROWS + ASTEPS + r] = jnp.zeros((LEV, 2 * W), f32)
+
+    arrive(h_e)
+    kind = jnp.where(me_o == 0, 1, jnp.where(me_o == no - 1, 2, 0))
+    spot = lax.rem(lane + 8, 24)
+    from_left = (lane >= 64) & (lane < 112) & (spot < 6)
+    from_right = (lane >= 64) & (lane < 112) & (spot >= 6) & (spot < 12)
+
+    def strip(e, lefts, rights, n):
+        place = 6 * (n % 4) + 48 * (n // 4)
+        return jnp.where(from_left, rolled(lefts, 64 - place), jnp.where(from_right, rolled(rights, 70 - place), e))
+
+    def strip_body(i, _):
+        for n in range(0, 8, 4):
+            made = []
+            for h in range(n, n + 4):
+                made.append(strip(own_e[8 * i + h], l_in[i], r_in[i], h))
+            at = 4 * i + n // 2 + ASTEPS // 2 + 1
+            put(sm, [at, at + 1], made, gf[kind])
+        return 0
+
+    lax.fori_loop(0, ROWS // 8, strip_body, 0)
+    for q in range(ASTEPS // 2):
+        made = []
+        for flat, first, corner, there in ((top_flat, 2, 0, me_a > 0), (bot_flat, 0, 2, me_a < na - 1)):
+            for h in range(2):
+                r = 2 * q + h if corner == 0 else ASTEPS - 2 - 2 * q + h
+                e0, e1 = beside_row(flat, 0, r + first), beside_row(flat, 1, r + first)
+                e = jnp.where((lane >= OWN) & (lane < 3 * OWN), rolled(e1, 2 * OWN), e0)
+                z = strip(e, d_in[corner], d_in[corner + 1], r + first)
+                made.append(jnp.where(there, z, 0.0))
+        put(sm, [q + 1, PAIRS - q], made, gf[kind], (ASTEPS - 2 * q - 1) // 2 * 2)
+    s6[0] = jnp.zeros((LEV, 2 * W), f32)
+    s6[PAIRS + 1] = jnp.zeros((LEV, 2 * W), f32)
+
+    d_strip = jnp.broadcast_to(eig[kind, pl.ds(1, 1), :], (LEV, W))
+    for k in range(ASTEPS - 1, -1, -1):
         ssrc, sdst = sm[k + 1], sm[k]
+        first = ASTEPS - k
 
         def strip_step(i, _):
             q = i + first // 2
@@ -456,76 +529,13 @@
         if k:
             @pl.when(me_a == 0)
             def _():
-                for r in range(ASTEPS):
-                    dst[r] = jnp.zeros((LEV, 2 * W), f32)
                 for r in range(ASTEPS // 2):
                     sdst[r + 1] = jnp.zeros((LEV, 2 * W), f32)
 
             @pl.when(me_a == na - 1)
             def _():
-                for r in range(ASTEPS):
-                    dst[ROWS + ASTEPS + r] = jnp.zeros((LEV, 2 * W), f32)
                 for r in range(ASTEPS // 2):
                     sdst[(ROWS + ASTEPS) // 2 + r + 1] = jnp.zeros((LEV, 2 * W), f32)
-
-    arrive(h_ob)
-    tall = BLK + 16
-    rr = rows_of((tall, W))
-    row_in = ((rr >= 8) | (me_a > 0)) & ((rr < BLK + 8) | (me_a < na - 1))
-    lane_t = lanes((tall, W))
-
-    def tall_of(c):
-        return jnp.concatenate([ob_top[c], ob[c], ob_bot[c]], 0)
-
-    def tall_edge(n, side):
-        body = oe_l[n] if side == 0 else oe_r[n]
-        return jnp.concatenate([oe_c[side, n], body, oe_c[2 + side, n]], 0)
-
-    def neighbours(x):
-        return (rolled(x, 1, 0) + rolled(x, tall - 1, 0)) + (rolled(x, 1) + rolled(x, W - 1))
-
-    def stepped(x, c0, c1):
-        for _ in range(OSTEPS):
-            x = c0 * x + c1 * neighbours(x)
-        return x
-
-    sea = jnp.where(row_in, tall_of(16), 0.0)
-    kap = tall_of(17)
-    c1 = kap * sea
-    c0 = sea - c1 * neighbours(sea)
-
-    def edges(own, l_edge, r_edge, at, slot):
-        out = jnp.where(lane_t < 32 * slot + 4, rolled(l_edge, 32 * slot - at), rolled(own, 32 * slot + 4))
-        out = jnp.where(lane_t >= 32 * slot + 16, rolled(own, 32 * slot + 24), out)
-        return jnp.where(lane_t >= 32 * slot + 24, rolled(r_edge, 32 * slot + 20 - at), out)
-
-    in_l = (lane_t >= 4) | (me_o > 0)
-    in_r = (lane_t < 24) | (me_o < no - 1)
-    used = ((lane_t < 12) | ((lane_t >= 16) & (lane_t < 28))) & in_l & in_r & row_in
-    tl, tr = tall_edge(1, 0), tall_edge(1, 1)
-    e_sea = jnp.where(used, edges(tall_of(16), tl, tr, 0, 0), 0.0)
-    e_kap = jnp.where(used, edges(kap, tl, tr, 8, 0), 0.0)
-
-    def four(x):
-        return (x + rolled(x, 32)) + (rolled(x, 64) + rolled(x, 96))
-
-    e_sea, e_kap = four(e_sea), four(e_kap)
-    e1 = e_kap * e_sea
-    e0 = e_sea - e1 * neighbours(e_sea)
-    ul, ur = tall_edge(0, 0), tall_edge(0, 1)
-    for g in range(4):
-        total = edges(tall_of(4 * g), ul, ur, 32 * g, 0)
-        for s in range(1, 4):
-            c = 4 * g + s
-            total = jnp.where(lane_t >= 32 * s, edges(tall_of(c), ul, ur, 8 * c, s), total)
-        st[g] = stepped(e_sea * total, e0, e1)[8:8 + BLK]
-    for c in range(16):
-        mid = stepped(sea * tall_of(c), c0, c1)[8:8 + BLK]
-        e = st[c // 4]
-        base = 32 * (c % 4)
-        mid = jnp.where(lane64 < 4, rolled(e, -base - 4), mid)
-        mid = jnp.where(lane64 >= W - 4, rolled(e, 104 - base), mid)
-        us[c] = mid + (1.0 - lf) * u_own[c]
 
     p_in[mine_rows] = p_out[mine_rows]
     arrive(g_p)
@@ -581,7 +591,7 @@
                 out_a[pl.ds(v * LEV * ROWS + x, LEV, stride=ROWS), :] = mids[2 * h + v] + extra[:, W * v:W * (v + 1)]
         return 0
 
-    lax.fori_loop(0, ROWS // 2, final_body, 0)
+    lax.fori_loop(0, ROWS // 2, final_body, 0, unroll=2)
     g_ao = local(out_a, atm_out, 5)
     for c in sent:
         c.wait_send()
@@ -605,7 +615,7 @@
 
     scratch = [
         v(2 * LEV * ROWS, W), v(2 * LEV, 8, W), v(2 * LEV, 8, W), v(2 * LEV * 8, W), v(2 * LEV * 8, W), v(16, BLK, W), v(BLK, W, W), v(BLK, W, W),
-        v(ROWS, LEV, W), v(11, LEV, W), v(11, LEV, W), v(11, LEV, W), v(4, 2, LEV, W),
+        v(ROWS, LEV, W), v(4, LEV, W), v(4, LEV, W), v(4, LEV, W), v(4, LEV, W), v(4, LEV, W),
         v(18, BLK, W), v(2, BLK, W), v(18, 8, W), v(18, 8, W), v(2, BLK, W), v(2, BLK, W), v(4, 2, 8, W),
         v(slots, W), v(slots, W), v(slots, 4 * W), v(slots, 4 * W), v(slots, 4 * W), v(slots, 4 * W),
         v(2, ROWS, W), v(2, ROWS, W), v(2, ROWS, W), v(2, 8, W), v(2, 8, W), v(4, 2, 8, W),

time: 68.4 us -> 54.7 us (0.80)
  Pallas kernels: 63.4 us -> 49.7 us
    pallas_call x1, Pallas kernels: 63.4 us -> 49.7 us  [shards(): pl.pallas_call(functools.partial(kernel, na, no, cap), out_shape=(jax.Sha...]
where the time goes in v2:
time: 54.7 us; the launch traced here: 54.5 us
  Pallas kernels  49.7 us (91%)
  local copies, waits for them, and re-layouts  4.13 us (8%)
  between operations  0.65 us (1%)
    pallas_call x1, Pallas kernels, shards(): pl.pallas_call(functools.partial(kernel, na, no, cap), out_shape=(jax.Sha...  49.7 us
    unnamed x4, local copies, waits for them, and re-layouts  4.13 us

profile of v2, /device:TPU:1, one launch (start us, length us, event | category | flops | bytes accessed | tf_op | source)
XLA Modules:
  0.0 54.5 jit_solution(15874304108480434217)
XLA Ops:
  0.6 49.7 %shard_map.185 = (f32[4608,128]{1,0:T(8,128)}, f32[16,64,128]{2,1,0:T(8,128)}) custom-call(f32[144,32,128]{2,1,0:T(8,128)} %bitcast.9, f32[4608,128]{1,0:T(8,128)} %bitcast.10, f32[16,64,128]{2,1,0:T(8,128)} %bitcast.12, s32[64,128]{1,0:T(8,128)} %land.1, f32[64,128]{1,0:T(8,128)} %kappa.1, s32[1,64]{1,0:T(1,128)} %bitcast.14, s32[1,64]{1,0:T(1,128)} %bitcast.15, ...), custom_call_target="tpu_custom_call" | custom-call | tf_op jit(solution)/shard_map/pallas_call | solution.py:629
  50.4 0.0 copy-start
  50.4 3.3 %copy.22 = f32[2,72,32,128]{3,2,1,0:T(8,128)} copy(f32[2,72,32,128]{3,2,1,0:T(8,128)} %bitcast.11) | data formatting | bytes 4718592
  53.7 0.0 copy-done
  53.7 0.8 %copy.23 = f32[4,4,64,128]{3,2,1,0:T(8,128)} copy(f32[4,4,64,128]{3,2,1,0:T(8,128)S(1)} %bitcast.13) | data formatting | bytes 1048576
Async XLA Ops:
  50.4 3.3 %copy-start = (f32[16,64,128]{2,1,0:T(8,128)S(1)}, f32[16,64,128]{2,1,0:T(8,128)}, u32[]{:S(2)}) copy-start(f32[16,64,128]{2,1,0:T(8,128)} %get-tuple-element.5) | copy-start | bytes 1572868

commit v3 on v2

--- a/solution.py
+++ b/solution.py
@@ -51,6 +51,17 @@
         if shift == 0:
             return x
     return pltpu.roll(x, shift, axis)
+
+
+def parts2(x):
+    hi = x.astype(bf16)
+    return hi, (x - hi.astype(f32)).astype(bf16)
+
+
+def changed(rows, matrix):
+    res = mm(jnp.concatenate(parts2(jnp.concatenate(rows, 0)), 1), matrix)
+    res = res[:, :W] + res[:, W:]
+    return [res[LEV * n:LEV * (n + 1)] for n in range(len(rows))]
 
 
 SEG = 3 * ASTEPS
@@ -110,14 +121,14 @@
 
 def kernel(
     na, no, cap,
-    atm, atm_flat, ocn, land, kappa, partner, prow, up, down, smix, drag, lk, vm, gain, qf, qi, gf, gi, eig,
-    atm_out, ocn_out,
+    atm, atm_flat, ocn, land, kappa, partner, prow, up, down, smix, drag, lk, vm, qf_all, gf_all, eig,
+    p_res, s_res, g_res, w_res, u_res, t_res,
     a_flat, a_top, a_bot, top_flat, bot_flat, u_own, up_v, down_v,
     own_e, r_out, l_out, l_in, r_in, d_in,
     ob, oe, ob_top, ob_bot, oe_l, oe_r, oe_c,
     rid_out, rid_in, c_out, c_in, p_out, p_in,
     fx, fx_l, fx_r, fx_t, fx_b, fx_c,
-    mx, cb, w_s, wf_s, gs, out_a, out_o, us, st,
+    mx, cb, w_s, wf_s, gs, us, st, term, qf, gf,
     p0, p1, p2, p3, p4, p5, p6,
     s0, s1, s2, s3, s4, s5, s6,
     loc, hs, hr, ps, pr,
@@ -140,7 +151,8 @@
     part = BLK // chunks
     g_up = [local(up.at[pl.ds(i * part, part)], up_v.at[pl.ds(i * part, part)], 1 + i) for i in range(chunks)]
     g_atm = local(atm_flat, a_flat, 5)
-    g_down = local(down, down_v, 6)
+    kind = jnp.where(me_o == 0, 1, jnp.where(me_o == no - 1, 2, 0))
+    g_qf = local(qf_all, qf, 7)
 
     barrier = pltpu.get_barrier_semaphore()
     greeted = [(me_a, lax.rem(me_o + d, no)) for d in range(1, no)]
@@ -150,6 +162,7 @@
     pl.semaphore_wait(barrier, len(greeted))
 
     sent = []
+    lane = lanes((LEV, W))
 
     def send(src, dst, i, r, c):
         d = pltpu.make_async_remote_copy(
@@ -222,64 +235,6 @@
     rid = jnp.sum(chosen * (r_row + 1.0), axis=1, keepdims=True) - 1.0
     rid_out[...] = jnp.broadcast_to(rid, (slots, W))
     g_rid = spread(rid_out, rid_in, 0)
-
-    for k in range(4):
-        total = smix[k, 0] * u_own[0]
-        for c in range(1, 16):
-            total = total + smix[k, c] * u_own[c]
-        total = total * lf
-        hi = high(total)
-        mx[pl.ds(k, BLK, stride=8), :] = hi
-        mx[pl.ds(4 + k, BLK, stride=8), :] = total - hi
-
-    def remap(b, weights, transposed):
-        block = weights[b]
-        hi = high(block)
-        parts = (hi.astype(bf16), (block - hi).astype(bf16))
-        vec = mx[pl.ds(pl.multiple_of(b * 8, 8), 8), :].astype(bf16)
-        if transposed:
-            res = mm(vec, jnp.concatenate(parts, 0), ((1,), (1,)))
-        else:
-            res = mm(vec, jnp.concatenate(parts, 1))
-        first = res[:, :W]
-        cb[pl.ds(pl.multiple_of(b * 8, 8), 8), :] = first + rolled(first, 4, 0) + res[:, W:]
-
-    for i in range(chunks):
-        g_up[i].wait()
-        lax.fori_loop(i * part, (i + 1) * part, lambda b, _: (remap(b, up_v, False), 0)[1], 0, unroll=4)
-    fields = jnp.concatenate([cb[pl.ds(k, BLK, stride=8), :] for k in range(4)], 1)
-    c_out[...] = pick(chosen, fields)
-    g_c = spread(c_out, c_in, 1)
-
-    g_atm.wait()
-    lane = lanes((LEV, W))
-
-    def own_row(v, x):
-        return a_flat[pl.ds(v * LEV * ROWS + x, LEV, stride=ROWS), :]
-
-    def gather(g, _):
-        to_r = to_l = jnp.zeros((LEV, W), f32)
-        for n in range(8):
-            x = 8 * g + n
-            e = jnp.where((lane >= OWN) & (lane < 3 * OWN), rolled(own_row(1, x), 2 * OWN), own_row(0, x))
-            own_e[x] = e
-            place = 6 * (n % 4) + 48 * (n // 4)
-            here = (lane // 48 == n // 4) & (lax.rem(lane, 24) // 6 == n % 4)
-            to_r = jnp.where(here, rolled(e, place + 6), to_r)
-            to_l = jnp.where(here, rolled(e, place), to_l)
-        r_out[g] = to_r
-        l_out[g] = to_l
-        return 0
-
-    lax.fori_loop(0, ROWS // 8, gather, 0)
-    h_e = [
-        send(r_out, l_in, 10, me_a, right),
-        send(l_out, r_in, 11, me_a, left),
-        send(r_out.at[3], d_in.at[0], 12, below, right),
-        send(l_out.at[3], d_in.at[1], 13, below, left),
-        send(r_out.at[0], d_in.at[2], 14, above, right),
-        send(l_out.at[0], d_in.at[3], 15, above, left),
-    ]
 
     exact = lax.Precision.HIGHEST
     rate = lk[...]
@@ -314,15 +269,70 @@
     chi = high(column)
     wf = chi + rolled(chi, 8) + rolled(column - chi, 16)
     wf_s[...] = jnp.concatenate([wf, jnp.zeros((8, W), f32)], 0)[:, :32].astype(bf16)
-
-    def parts2(x):
-        hi = x.astype(bf16)
-        return hi, (x - hi.astype(f32)).astype(bf16)
-
-    def changed(rows, matrix):
-        res = mm(jnp.concatenate(parts2(jnp.concatenate(rows, 0)), 1), matrix)
-        res = res[:, :W] + res[:, W:]
-        return [res[LEV * n:LEV * (n + 1)] for n in range(len(rows))]
+    done = [local(wf_s, w_res, 9)]
+
+    for k in range(4):
+        total = smix[k, 0] * u_own[0]
+        for c in range(1, 16):
+            total = total + smix[k, c] * u_own[c]
+        total = total * lf
+        hi = high(total)
+        mx[pl.ds(k, BLK, stride=8), :] = hi
+        mx[pl.ds(4 + k, BLK, stride=8), :] = total - hi
+
+    def remap(b, weights, transposed):
+        block = weights[b]
+        hi = high(block)
+        parts = (hi.astype(bf16), (block - hi).astype(bf16))
+        vec = mx[pl.ds(pl.multiple_of(b * 8, 8), 8), :].astype(bf16)
+        if transposed:
+            res = mm(vec, jnp.concatenate(parts, 0), ((1,), (1,)))
+        else:
+            res = mm(vec, jnp.concatenate(parts, 1))
+        first = res[:, :W]
+        cb[pl.ds(pl.multiple_of(b * 8, 8), 8), :] = first + rolled(first, 4, 0) + res[:, W:]
+
+    def own_row(v, x):
+        return a_flat[pl.ds(v * LEV * ROWS + x, LEV, stride=ROWS), :]
+
+    def gather(g, _):
+        to_r = to_l = jnp.zeros((LEV, W), f32)
+        for n in range(8):
+            x = 8 * g + n
+            e = jnp.where((lane >= OWN) & (lane < 3 * OWN), rolled(own_row(1, x), 2 * OWN), own_row(0, x))
+            own_e[x] = e
+            place = 6 * (n % 4) + 48 * (n // 4)
+            here = (lane // 48 == n // 4) & (lax.rem(lane, 24) // 6 == n % 4)
+            to_r = jnp.where(here, rolled(e, place + 6), to_r)
+            to_l = jnp.where(here, rolled(e, place), to_l)
+        r_out[g] = to_r
+        l_out[g] = to_l
+
+    def gather_remap(g, _):
+        for n in range(16):
+            remap(16 * g + n, up_v, False)
+        gather(g, _)
+        return 0
+
+    for i in range(chunks):
+        g_up[i].wait()
+    g_atm.wait()
+    lax.fori_loop(0, 4, gather_remap, 0)
+    g_gf = local(gf_all.at[kind], gf, 8)
+    g_down = local(down, down_v, 6)
+    fields = jnp.concatenate([cb[pl.ds(k, BLK, stride=8), :] for k in range(4)], 1)
+    c_out[...] = pick(chosen, fields)
+    g_c = spread(c_out, c_in, 1)
+
+
+    h_e = [
+        send(r_out, l_in, 10, me_a, right),
+        send(l_out, r_in, 11, me_a, left),
+        send(r_out.at[3], d_in.at[0], 12, below, right),
+        send(l_out.at[3], d_in.at[1], 13, below, left),
+        send(r_out.at[0], d_in.at[2], 14, above, right),
+        send(l_out.at[0], d_in.at[3], 15, above, left),
+    ]
 
     def powers(x, low=0):
         hi = high(x)
@@ -396,6 +406,8 @@
         mid = jnp.where(lane64 >= W - 4, rolled(e, lax.rem(W + 104 - 32 * slot, W)), mid)
         us[c] = mid + (1.0 - lf) * u_own[c]
 
+    g_qf.wait()
+
     def own_body(i, _):
         xs = [4 * i + n for n in range(4)]
         put(pm, [x + ASTEPS for x in xs], [own_row(v, x) for x in xs for v in range(2)], qf[...])
@@ -405,6 +417,8 @@
         return 0
 
     lax.fori_loop(0, ROWS // 4, own_body, 0)
+
+    done.append(local(us, u_res, 10))
 
     rid_in[mine_rows] = rid_out[mine_rows]
     c_in[mine_rows] = c_out[mine_rows]
@@ -480,8 +494,10 @@
                 for r in range(ASTEPS):
                     dst[ROWS + ASTEPS + r] = jnp.zeros((LEV, 2 * W), f32)
 
+    done.append(local(p0.at[pl.ds(ASTEPS, ROWS)], p_res, 11))
+
     arrive(h_e)
-    kind = jnp.where(me_o == 0, 1, jnp.where(me_o == no - 1, 2, 0))
+    g_gf.wait()
     spot = lax.rem(lane + 8, 24)
     from_left = (lane >= 64) & (lane < 112) & (spot < 6)
     from_right = (lane >= 64) & (lane < 112) & (spot >= 6) & (spot < 12)
@@ -496,7 +512,7 @@
             for h in range(n, n + 4):
                 made.append(strip(own_e[8 * i + h], l_in[i], r_in[i], h))
             at = 4 * i + n // 2 + ASTEPS // 2 + 1
-            put(sm, [at, at + 1], made, gf[kind])
+            put(sm, [at, at + 1], made, gf[...])
         return 0
 
     lax.fori_loop(0, ROWS // 8, strip_body, 0)
@@ -509,7 +525,7 @@
                 e = jnp.where((lane >= OWN) & (lane < 3 * OWN), rolled(e1, 2 * OWN), e0)
                 z = strip(e, d_in[corner], d_in[corner + 1], r + first)
                 made.append(jnp.where(there, z, 0.0))
-        put(sm, [q + 1, PAIRS - q], made, gf[kind], (ASTEPS - 2 * q - 1) // 2 * 2)
+        put(sm, [q + 1, PAIRS - q], made, gf[...], (ASTEPS - 2 * q - 1) // 2 * 2)
     s6[0] = jnp.zeros((LEV, 2 * W), f32)
     s6[PAIRS + 1] = jnp.zeros((LEV, 2 * W), f32)
 
@@ -536,6 +552,8 @@
             def _():
                 for r in range(ASTEPS // 2):
                     sdst[(ROWS + ASTEPS) // 2 + r + 1] = jnp.zeros((LEV, 2 * W), f32)
+
+    done.append(local(s0.at[pl.ds(ASTEPS // 2 + 1, ROWS // 2)], s_res, 12))
 
     p_in[mine_rows] = p_out[mine_rows]
     arrive(g_p)
@@ -548,10 +566,8 @@
     g_down.wait()
     lax.fori_loop(0, BLK, lambda b, _: (remap(b, down_v, True), 0)[1], 0, unroll=4)
     for v in range(4):
-        term = cb[pl.ds(v, BLK, stride=8), :] * lf
-        for n in range(4):
-            out_o[4 * v + n] = us[4 * v + n] + gain[0, n] * term
-    g_oo = local(out_o, ocn_out, 0)
+        term[v] = cb[pl.ds(v, BLK, stride=8), :] * lf
+    done.append(local(term, t_res, 13))
 
     arrive(h_f)
     rows48, lanes384 = rows_of((ROWS + 16, 3 * W)), lanes((ROWS + 16, 3 * W))
@@ -573,30 +589,29 @@
                 cur = grid_in * (
                     (rolled(cur, 1, 0) + rolled(cur, ROWS + 15, 0)) + (rolled(cur, 1) + rolled(cur, 3 * W - 1))
                 )
-
-    def final_body(i, _):
-        mids = [p0[2 * i + h + ASTEPS, :, W * v:W * (v + 1)] for h in range(2) for v in range(2)]
-        mids = changed(mids, qi[...])
-        e = s0[i + ASTEPS // 2 + 1]
-        hi, mid = parts2(jnp.concatenate([e[:, :W], e[:, W:]], 0))
-        side = mm(jnp.concatenate([hi, mid, hi], 1), gi[kind])
-        for h in range(2):
-            x = 2 * i + h
-            at = pl.ds(pl.multiple_of(8 * x, 8), 8)
-            g = jnp.concatenate([gs[0, at, :], gs[1, at, :]], 1)
-            hi = high(g)
-            rhs = jnp.concatenate([hi, g - hi, hi, jnp.zeros((8, 2 * W), f32)], 0).astype(bf16)
-            extra = mm(wf_s[...], rhs)[:LEV] + side[LEV * h:LEV * (h + 1)]
-            for v in range(2):
-                out_a[pl.ds(v * LEV * ROWS + x, LEV, stride=ROWS), :] = mids[2 * h + v] + extra[:, W * v:W * (v + 1)]
-        return 0
-
-    lax.fori_loop(0, ROWS // 2, final_body, 0, unroll=2)
-    g_ao = local(out_a, atm_out, 5)
+    done.append(local(gs, g_res, 14))
     for c in sent:
         c.wait_send()
-    g_oo.wait()
-    g_ao.wait()
+    for c in done:
+        c.wait()
+
+
+def finish(no, rows, tile, side, powers, wf, ocean, term, gain, qi, gi, air_out, ocean_out, flat):
+    me_o = lax.axis_index("ocn")
+    kind = jnp.where(me_o == 0, 1, jnp.where(me_o == no - 1, 2, 0))
+    mids = changed([tile[x, :, W * v:W * (v + 1)] for x in range(rows) for v in range(2)], qi[...])
+    hi, mid = parts2(jnp.concatenate([side[x // 2, :, W * (x % 2):W * (x % 2 + 1)] for x in range(rows)], 0))
+    beside = mm(jnp.concatenate([hi, mid, hi], 1), gi[kind])
+    for x in range(rows):
+        g = jnp.concatenate([powers[v, 8 * x:8 * x + 8, :] for v in range(2)], 1)
+        hi = high(g)
+        rhs = jnp.concatenate([hi, g - hi, hi, jnp.zeros((8, 2 * W), f32)], 0).astype(bf16)
+        extra = mm(wf[...], rhs)[:LEV] + beside[LEV * x:LEV * (x + 1)]
+        for v in range(2):
+            flat[pl.ds(v * LEV * rows + x, LEV, stride=rows), :] = mids[2 * x + v] + extra[:, W * v:W * (v + 1)]
+    air_out[...] = flat[...].reshape(2 * LEV, rows, W)
+    for n in range(4):
+        ocean_out[n] = ocean[n] + gain[0, n] * term[0]
 
 
 def shards(
@@ -620,20 +635,26 @@
         v(slots, W), v(slots, W), v(slots, 4 * W), v(slots, 4 * W), v(slots, 4 * W), v(slots, 4 * W),
         v(2, ROWS, W), v(2, ROWS, W), v(2, ROWS, W), v(2, 8, W), v(2, 8, W), v(4, 2, 8, W),
         v(BLK * 8, W), v(BLK * 8, W), v(512, 240, dtype=bf16), v(80, 32, dtype=bf16), v(2, ROWS * 8, W),
-        v(2 * LEV * ROWS, W), v(16, BLK, W), v(16, BLK, W), v(4, BLK, W),
+        v(16, BLK, W), v(4, BLK, W), v(4, BLK, W),
+        v(2 * W, 2 * W, dtype=bf16), v(2 * W, 2 * W, dtype=bf16),
     ]
     scratch += [v(EXT, LEV, 2 * W) for _ in range(7)]
     scratch += [v(PAIRS + 2, LEV, 2 * W) for _ in range(7)]
     dma = pltpu.SemaphoreType.DMA
-    scratch += [dma((7,)), dma((24,)), dma((24,)), dma((3, no)), dma((3, no))]
-    air, sea = pl.pallas_call(
+    scratch += [dma((15,)), dma((24,)), dma((24,)), dma((3, no)), dma((3, no))]
+    q_there, q_back, g_there, g_back, eig = [jnp.asarray(m) for m in transforms()]
+
+    def out(*shape, dtype=f32):
+        return jax.ShapeDtypeStruct(shape, dtype)
+
+    tile, side, powers, wf, ocean, term = pl.pallas_call(
         functools.partial(kernel, na, no, cap),
         out_shape=(
-            jax.ShapeDtypeStruct((2 * LEV * ROWS, W), f32),
-            jax.ShapeDtypeStruct((16, BLK, W), f32),
+            out(ROWS, LEV, 2 * W), out(ROWS // 2, LEV, 2 * W), out(2, ROWS * 8, W), out(80, 32, dtype=bf16),
+            out(16, BLK, W), out(4, BLK, W),
         ),
-        in_specs=[hbm, hbm, hbm, vmem, vmem, vmem, vmem, hbm, hbm, smem, vmem, vmem, vmem, smem] + [vmem] * 5,
-        out_specs=(hbm, hbm),
+        in_specs=[hbm, hbm, hbm, vmem, vmem, vmem, vmem, hbm, hbm, smem, vmem, vmem, vmem, hbm, hbm, vmem],
+        out_specs=(hbm,) * 6,
         scratch_shapes=scratch,
         compiler_params=pltpu.CompilerParams(
             collective_id=0, has_side_effects=True, vmem_limit_bytes=63 * 1024 * 1024
@@ -652,9 +673,34 @@
         drag,
         level_kappa.reshape(1, LEV),
         vertical_mix,
-        depth_gain.reshape(1, 4),
-        *[jnp.asarray(m) for m in transforms()],
+        q_there,
+        g_there,
+        eig,
     )
+    rows = 8
+    whole = pl.BlockSpec(memory_space=pltpu.VMEM)
+    air, sea = pl.pallas_call(
+        functools.partial(finish, no, rows),
+        grid=(ROWS // rows,),
+        out_shape=(out(2 * LEV, ROWS, W), out(16, BLK, W)),
+        in_specs=[
+            pl.BlockSpec((rows, LEV, 2 * W), lambda i: (i, 0, 0)),
+            pl.BlockSpec((rows // 2, LEV, 2 * W), lambda i: (i, 0, 0)),
+            pl.BlockSpec((2, rows * 8, W), lambda i: (0, i, 0)),
+            whole,
+            pl.BlockSpec((4, BLK, W), lambda i: (i, 0, 0)),
+            pl.BlockSpec((1, BLK, W), lambda i: (i, 0, 0)),
+            smem,
+            whole,
+            whole,
+        ],
+        out_specs=(
+            pl.BlockSpec((2 * LEV, rows, W), lambda i: (0, i, 0)),
+            pl.BlockSpec((4, BLK, W), lambda i: (i, 0, 0)),
+        ),
+        scratch_shapes=[v(2 * LEV * rows, W)],
+        compiler_params=pltpu.CompilerParams(vmem_limit_bytes=63 * 1024 * 1024),
+    )(tile, side, powers, wf, ocean, term, depth_gain.reshape(1, 4), q_back, g_back)
     return air.reshape(atm_state.shape), sea.reshape(ocn_state.shape)
 
 

time: 54.7 us -> 48.5 us (0.89)
  local copies, waits for them, and re-layouts: 4.13 us -> 0 us
  Pallas kernels: 49.7 us -> 47.6 us
    unnamed x4 -> x0, local copies, waits for them, and re-layouts: 4.13 us -> none
    pallas_call x1 -> x2, Pallas kernels: 49.7 us -> 47.6 us  [the longest x1 41.8 us: shards(): pl.pallas_call(functools.partial(kernel, na, no, cap), out_shape=(out(ROW...]
where the time goes in v3:
time: 48.5 us; the launch traced here: 48.2 us
  Pallas kernels  47.6 us (98%)
  between operations  0.64 us (1%)
    pallas_call x1, Pallas kernels, shards(): pl.pallas_call(functools.partial(kernel, na, no, cap), out_shape=(out(ROW...  41.8 us
    pallas_call x1, Pallas kernels, shards(): pl.pallas_call(functools.partial(finish, no, rows), grid=(ROWS // rows,),...  5.8 us

profile of v3, /device:TPU:1, one launch (start us, length us, event | category | flops | bytes accessed | tf_op | source)
XLA Modules:
  0.0 48.2 jit_solution(5085229745610640897)
XLA Ops:
  0.6 41.8 %shard_map.185 = (f32[32,72,256]{2,1,0:T(8,128)}, f32[16,72,256]{2,1,0:T(8,128)}, f32[2,256,128]{2,1,0:T(8,128)}, bf16[80,32]{1,0:T(8,128)(2,1)}, f32[16,64,128]{2,1,0:T(8,128)}, /*index=5*/f32[4,64,128]{2,1,0:T(8,128)}) custom-call(f32[144,32,128]{2,1,0:T(8,128)} %bitcast.9, f32[4608,128]{1,0:T(8,128)} %bitcast.10, f32[16,64,128]{2,1,0:T(8,128)} %bitcast.11, ...), custom_call_target="tpu_custom_call" | custom-call | tf_op jit(solution)/shard_map/pallas_call | solution.py:650
  42.4 5.8 %shard_map.186 = (f32[144,32,128]{2,1,0:T(8,128)}, f32[16,64,128]{2,1,0:T(8,128)}) custom-call(f32[32,72,256]{2,1,0:T(8,128)} %get-tuple-element.10.tile, f32[16,72,256]{2,1,0:T(8,128)} %get-tuple-element.11.side, f32[2,256,128]{2,1,0:T(8,128)} %get-tuple-element.12.powers, bf16[80,32]{1,0:T(8,128)(2,1)} %get-tuple-element.13.wf, ...), custom_call_target="tpu_custom_call" | custom-call | tf_op jit(solution)/shard_map/pallas_call | solution.py:682

commit v4 on v3

--- a/solution.py
+++ b/solution.py
@@ -416,7 +416,7 @@
             channel(2 * i + h, st[lax.div(i, 2)], slot)
         return 0
 
-    lax.fori_loop(0, ROWS // 4, own_body, 0)
+    lax.fori_loop(0, ROWS // 4, own_body, 0, unroll=4)
 
     done.append(local(us, u_res, 10))
 
@@ -481,7 +481,7 @@
                 for n in range(group):
                     dst[r + n, :, sl] = made[n]
             return 0
-        lax.fori_loop(0, count // group, main_body, 0)
+        lax.fori_loop(0, count // group, main_body, 0, unroll=2 if count // group % 2 == 0 else 1)
 
         if k:
             @pl.when(me_a == 0)
@@ -515,7 +515,7 @@
             put(sm, [at, at + 1], made, gf[...])
         return 0
 
-    lax.fori_loop(0, ROWS // 8, strip_body, 0)
+    lax.fori_loop(0, ROWS // 8, strip_body, 0, unroll=2)
     for q in range(ASTEPS // 2):
         made = []
         for flat, first, corner, there in ((top_flat, 2, 0, me_a > 0), (bot_flat, 0, 2, me_a < na - 1)):
@@ -540,7 +540,7 @@
             sdst[q + 1, :, :W] = sdst[q + 1, :, :W] + ((ssrc[q, :, W:] + a1) + d_strip * a0)
             sdst[q + 1, :, W:] = sdst[q + 1, :, W:] + ((ssrc[q + 2, :, :W] + a0) + d_strip * a1)
             return 0
-        lax.fori_loop(0, PAIRS - 2 * (first // 2), strip_step, 0)
+        lax.fori_loop(0, PAIRS - 2 * (first // 2), strip_step, 0, unroll=2)
 
         if k:
             @pl.when(me_a == 0)
@@ -564,7 +564,7 @@
         mx[pl.ds(k, BLK, stride=8), :] = hi
         mx[pl.ds(4 + k, BLK, stride=8), :] = x - hi
     g_down.wait()
-    lax.fori_loop(0, BLK, lambda b, _: (remap(b, down_v, True), 0)[1], 0, unroll=4)
+    lax.fori_loop(0, BLK, lambda b, _: (remap(b, down_v, True), 0)[1], 0, unroll=16)
     for v in range(4):
         term[v] = cb[pl.ds(v, BLK, stride=8), :] * lf
     done.append(local(term, t_res, 13))
@@ -610,8 +610,8 @@
         for v in range(2):
             flat[pl.ds(v * LEV * rows + x, LEV, stride=rows), :] = mids[2 * x + v] + extra[:, W * v:W * (v + 1)]
     air_out[...] = flat[...].reshape(2 * LEV, rows, W)
-    for n in range(4):
-        ocean_out[n] = ocean[n] + gain[0, n] * term[0]
+    for n in range(16 * rows // ROWS):
+        ocean_out[n] = ocean[n] + gain[0, n % 4] * term[n // 4]
 
 
 def shards(
@@ -677,7 +677,7 @@
         g_there,
         eig,
     )
-    rows = 8
+    rows = 16
     whole = pl.BlockSpec(memory_space=pltpu.VMEM)
     air, sea = pl.pallas_call(
         functools.partial(finish, no, rows),
@@ -688,15 +688,15 @@
             pl.BlockSpec((rows // 2, LEV, 2 * W), lambda i: (i, 0, 0)),
             pl.BlockSpec((2, rows * 8, W), lambda i: (0, i, 0)),
             whole,
-            pl.BlockSpec((4, BLK, W), lambda i: (i, 0, 0)),
-            pl.BlockSpec((1, BLK, W), lambda i: (i, 0, 0)),
+            pl.BlockSpec((16 * rows // ROWS, BLK, W), lambda i: (i, 0, 0)),
+            pl.BlockSpec((4 * rows // ROWS, BLK, W), lambda i: (i, 0, 0)),
             smem,
             whole,
             whole,
         ],
         out_specs=(
             pl.BlockSpec((2 * LEV, rows, W), lambda i: (0, i, 0)),
-            pl.BlockSpec((4, BLK, W), lambda i: (i, 0, 0)),
+            pl.BlockSpec((16 * rows // ROWS, BLK, W), lambda i: (i, 0, 0)),
         ),
         scratch_shapes=[v(2 * LEV * rows, W)],
         compiler_params=pltpu.CompilerParams(vmem_limit_bytes=63 * 1024 * 1024),

time: 48.5 us -> 44.7 us (0.922)
  Pallas kernels: 47.6 us -> 43.8 us
    pallas_call x1, Pallas kernels: 41.8 us -> 38.2 us  [shards(): pl.pallas_call(functools.partial(kernel, na, no, cap), out_shape=(out(ROW...]
where the time goes in v4:
time: 44.7 us; the launch traced here: 44.5 us
  Pallas kernels  43.8 us (98%)
  between operations  0.64 us (1%)
    pallas_call x1, Pallas kernels, shards(): pl.pallas_call(functools.partial(kernel, na, no, cap), out_shape=(out(ROW...  38.2 us
    pallas_call x1, Pallas kernels, shards(): pl.pallas_call(functools.partial(finish, no, rows), grid=(ROWS // rows,),...  5.67 us

profile of v4, /device:TPU:1, one launch (start us, length us, event | category | flops | bytes accessed | tf_op | source)
XLA Modules:
  0.0 44.5 jit_solution(15339679015802633961)
XLA Ops:
  0.6 38.2 %shard_map.185 = (f32[32,72,256]{2,1,0:T(8,128)}, f32[16,72,256]{2,1,0:T(8,128)}, f32[2,256,128]{2,1,0:T(8,128)}, bf16[80,32]{1,0:T(8,128)(2,1)}, f32[16,64,128]{2,1,0:T(8,128)}, /*index=5*/f32[4,64,128]{2,1,0:T(8,128)}) custom-call(f32[144,32,128]{2,1,0:T(8,128)} %bitcast.9, f32[4608,128]{1,0:T(8,128)} %bitcast.10, f32[16,64,128]{2,1,0:T(8,128)} %bitcast.11, ...), custom_call_target="tpu_custom_call" | custom-call | tf_op jit(solution)/shard_map/pallas_call | solution.py:650
  38.8 5.7 %shard_map.186 = (f32[144,32,128]{2,1,0:T(8,128)}, f32[16,64,128]{2,1,0:T(8,128)}) custom-call(f32[32,72,256]{2,1,0:T(8,128)} %get-tuple-element.10.tile, f32[16,72,256]{2,1,0:T(8,128)} %get-tuple-element.11.side, f32[2,256,128]{2,1,0:T(8,128)} %get-tuple-element.12.powers, bf16[80,32]{1,0:T(8,128)(2,1)} %get-tuple-element.13.wf, ...), custom_call_target="tpu_custom_call" | custom-call | tf_op jit(solution)/shard_map/pallas_call | solution.py:682
